TPU v7x, 256 devices: a whole 4x4x8 slice. The times are simulated.
256 devices in a mesh: clus: 16 (over z, core), sub: 16 (over y, x).
Axes of the slice: x: 4, y: 4, z: 8, core: 2. Of those that a mesh axis runs over, the one named last changes fastest.
Arguments:
- right_side: float32 [16, 16, 896, 512], P('clus', 'sub'), may hold values from -6 to 6
- dual_operator: float32 [16, 16, 896, 896], P('clus', 'sub'), may hold values from -1 to 3
- corner_basis: float32 [16, 16, 24, 896], P('clus', 'sub'), may hold values from -0.1875 to 0.1875
- coarse_inverse: float32 [16, 384, 384], P('clus'), may hold values from -1 to 2
- corner_map: int32 [16, 384], P('clus'), may hold values from 0 to 383, each once within a row
- iface_counts: int32 [16, 16, 16], P('clus', 'sub'), may hold values from 0 to 16, as said below
Outputs:
- solution: float32 [16, 16, 896, 512], P('clus', 'sub')
- residual: float32 [16, 16, 896, 512], P('clus', 'sub')
Inputs may be any that keep to these rules, and one draw needn't show every extreme that they name: `iface_counts`: symmetric in its last two dimensions with a zero diagonal; in every cluster one subdomain shares exactly 16 multipliers with every other subdomain of the cluster.
All inputs are finite; a program needn't handle non-finite values.
Results may differ from a plain program's by a relative error of at most 0.00011.
Values sent between devices are 32-bit elements; how exact they have to be, the bound alone decides.
No kernel may reach another device: no remote copies, remote signals or barrier semaphores. Data moves between devices by JAX's collectives and lax.ppermute only.
A program may use at most 64 MiB of HBM per device.

v0:
```python
import jax
import jax.numpy as jnp
from jax import lax
from jax.experimental import pallas as pl
from jax.experimental.pallas import tpu as pltpu
from jax.sharding import PartitionSpec as P

LOC = 896
NCOR = 24
NPAD = 32
XC = 128
FACE = 2 * XC
CAP = 16
SUBS = 16
MID = SUBS * CAP
SPAN = CAP + 8
ITERS = 3
COARSE = SUBS * NCOR
ROWS = CAP + NCOR
WIDE = 256

spectrum_low = 0.5
spectrum_high = 3.0
center_value = (spectrum_high + spectrum_low) / 2.0
half_width = (spectrum_high - spectrum_low) / 2.0
sigma_one = center_value / half_width

BF = jnp.bfloat16
F32 = jnp.float32
SM = pl.BlockSpec(memory_space=pltpu.SMEM)
ANY = pl.BlockSpec(memory_space=pl.ANY)
VM = pl.BlockSpec(memory_space=pltpu.VMEM)


def split(x):
    hi = x.astype(BF)
    return hi, (x - hi.astype(F32)).astype(BF)


def mm(a, b):
    return jnp.dot(a, b, preferred_element_type=F32)


def mm3(ahi, alo, bhi, blo):
    return mm(ahi, bhi) + (mm(ahi, blo) + mm(alo, bhi))


def sds(shape, dtype=F32):
    return jax.ShapeDtypeStruct(shape, dtype)


def call(body, outs, ins, specs, scratch, copies, flops):
    return pl.pallas_call(
        body,
        out_shape=outs,
        in_specs=specs,
        out_specs=tuple(ANY for _ in outs),
        scratch_shapes=tuple(pltpu.VMEM(*s) for s in scratch) + (pltpu.SemaphoreType.DMA((copies,)),),
        compiler_params=pltpu.CompilerParams(vmem_limit_bytes=56 * 1024 * 1024),
        cost_estimate=pl.CostEstimate(flops=flops, bytes_accessed=6_000_000, transcendentals=0),
    )(*ins)


class Copies:
    def __init__(self, sems):
        self.sems, self.used, self.open = sems, 0, []

    def get(self, source, target):
        copy = pltpu.make_async_copy(source, target, self.sems.at[self.used])
        self.used += 1
        copy.start()
        return copy

    def put(self, source, target):
        self.open.append(self.get(source, target))

    def finish(self):
        for copy in self.open:
            copy.wait()


def face_starts(counts):
    starts, at = [], 0
    for p in range(SUBS):
        starts.append(at)
        at = at + counts[0, p]
    return starts, at


def place(at):
    low = lax.rem(at, 8)
    return pl.ds(pl.multiple_of(at - low, 8), SPAN), low


def take_rows(source, at):
    if isinstance(at, int):
        return source[at : at + CAP]
    window, low = place(at)
    return pltpu.roll(source[window, :], lax.rem(SPAN - low, SPAN), 0)[:CAP]


def put_rows(target, at, rows):
    if isinstance(at, int):
        target[at : at + CAP] = rows
        return
    window, low = place(at)
    moved = pltpu.roll(jnp.concatenate([rows, rows[:8]], axis=0), low, 0)
    keep = lax.broadcasted_iota(jnp.int32, moved.shape, 0) >= low
    target[window, :] = jnp.where(keep, moved, target[window, :])


def columns(width):
    return [pl.ds(at, WIDE) for at in range(0, width, WIDE)]


def fill(out, cols, product):
    for p in range(SUBS):
        out[p, :CAP, cols] = product[p * CAP : (p + 1) * CAP]
        out[p, CAP:, cols] = product[MID : MID + NCOR]


def padded(basis):
    return jnp.concatenate([basis, jnp.zeros((NPAD - NCOR, basis.shape[1]), F32)], axis=0)


def even_cluster():
    return lax.rem(lax.axis_index("clus"), 2) == 0


def pick(near, far):
    even = even_cluster()
    return jnp.where(even, far, near), jnp.where(even, near, far)


def sent_rows(flow, blocks, mhi_v, mlo_v, ends_v, dhi_v, dlo_v, out, near, far, out_v, near_v, far_v, prepare):
    for at, cols in enumerate(blocks):
        prepare(at, cols)
        fill(out_v, cols, mm3(mhi_v[...], mlo_v[...], dhi_v[:, cols], dlo_v[:, cols]))
        flow.put(out_v.at[:, :, cols], out.at[:, :, cols])
    prepare(len(blocks), None)
    zhi, zlo = split(ends_v[...])
    for cols in blocks:
        product = mm3(zhi, zlo, dhi_v[:, cols], dlo_v[:, cols])
        far_v[:, cols], near_v[:, cols] = pick(product[XC:], product[:XC])
        flow.put(far_v.at[:, cols], far.at[:, cols])
        flow.put(near_v.at[:, cols], near.at[:, cols])
    flow.finish()


def first_body(rhs, op, basis, counts, out, near, far, mhi, mlo, rhs_v, held, ends_v, basis_v, out_v, near_v, far_v, mhi_v, mlo_v, dhi_v, dlo_v, sems):
    flow = Copies(sems)
    rows_in = flow.get(op.at[pl.ds(FACE, MID + 8)], held)
    basis_in = flow.get(basis, basis_v)
    blocks = columns(rhs.shape[1])
    rhs_in = [flow.get(rhs.at[:, cols], rhs_v.at[:, cols]) for cols in blocks]
    ends_in = flow.get(op.at[pl.ds(0, FACE)], ends_v)
    basis_in.wait()
    mhi_v[MID:], mlo_v[MID:] = split(padded(basis_v[...]))
    starts, _ = face_starts(counts)
    rows_in.wait()
    for p in range(SUBS):
        rows = slice(p * CAP, (p + 1) * CAP)
        mhi_v[rows], mlo_v[rows] = split(take_rows(held, starts[p]))
    flow.put(mhi_v, mhi)
    flow.put(mlo_v, mlo)

    def prepare(at, cols):
        if cols is None:
            ends_in.wait()
        else:
            rhs_in[at].wait()
            dhi_v[:, cols], dlo_v[:, cols] = split(rhs_v[:, cols] * (1.0 / center_value))

    sent_rows(flow, blocks, mhi_v, mlo_v, ends_v, dhi_v, dlo_v, out, near, far, out_v, near_v, far_v, prepare)


def landed_body(near_in, far_in, edge, sems):
    flow = Copies(sems)
    even = even_cluster()
    near_at = pl.multiple_of(jnp.where(even, XC, 0), XC)
    far_at = pl.multiple_of(jnp.where(even, 0, XC), XC)
    flow.put(near_in, edge.at[pl.ds(near_at, XC)])
    flow.put(far_in, edge.at[pl.ds(far_at, XC)])
    flow.finish()


def table_rows(inverse_v, places, place_v, rows):
    own = lax.axis_index("sub") * NCOR
    rows[NCOR:] = jnp.zeros((NPAD - NCOR, COARSE), F32)
    for n in range(NCOR):
        rows[n : n + 1] = inverse_v[pl.ds(places[0, own + n], 1), :]
    chosen = lax.broadcasted_iota(jnp.int32, (COARSE, COARSE), 0) == place_v[...]
    chosen = jnp.where(chosen, 1.0, 0.0).astype(BF)
    top, mid = split(rows[...])
    low = (rows[...] - top.astype(F32) - mid.astype(F32)).astype(BF)
    return mm(top, chosen) + (mm(mid, chosen) + mm(low, chosen))


def table_body(inverse, places, place_row, basis, table, turned, inverse_v, place_v, basis_v, rows, table_v, turned_v, sems):
    flow = Copies(sems)
    inverse_in = [flow.get(inverse, inverse_v), flow.get(place_row, place_v)]
    basis_in = flow.get(basis, basis_v)
    for copy in inverse_in:
        copy.wait()
    table_v[:NPAD], table_v[NPAD:] = split(table_rows(inverse_v, places, place_v, rows))
    flow.put(table_v, table)
    basis_in.wait()
    bhi, blo = split(padded(basis_v[...]).T)
    turned_v[...] = jnp.concatenate([bhi, bhi, blo], axis=1)
    flow.put(turned_v, turned)
    flow.finish()


HALF = (LOC - FACE) // 2
CHUNKS = (pl.ds(FACE, HALF), pl.ds(FACE + HALF, HALF))


def rest_body(in_scale, new_by, old_by, product_by, last):
    olds = 0 if old_by is None else 2 if last else 1

    def body(op, near, far, dirn, *refs):
        before, refs = refs[:olds], refs[olds:]
        outs, refs = refs[: 1 + last], refs[1 + last :]
        (op_v, near_v, far_v, dirn_v), refs = refs[:4], refs[4:]
        before_v, made, sems = refs[:olds], refs[olds:-1], refs[-1]
        flow = Copies(sems)
        blocks = columns(dirn.shape[1])
        op_in, dirn_in, before_in = [], [], []
        for at, cols in enumerate(blocks):
            dirn_in.append(flow.get(dirn.at[:, cols], dirn_v.at[:, cols]))
            if at == 0:
                op_in.append(flow.get(op.at[CHUNKS[0]], op_v.at[CHUNKS[0]]))
            before_in.append([flow.get(x.at[:, cols], y.at[:, cols]) for x, y in zip(before, before_v)])
            if at == 0:
                op_in.append(flow.get(op.at[CHUNKS[1]], op_v.at[CHUNKS[1]]))
                edges_in = [flow.get(near, near_v), flow.get(far, far_v)]
        factors = []
        for at, cols in enumerate(blocks):
            dirn_in[at].wait()
            dhi, dlo = split(dirn_v[:, cols] * in_scale)

            def store(rows, product):
                value = new_by * dirn_v[rows, cols] - product_by * product
                if olds:
                    value = value + old_by * before_v[0][rows, cols]
                made[0][rows, cols] = value
                flow.put(made[0].at[rows, cols], outs[0].at[rows, cols])

            for part, rows in enumerate(CHUNKS):
                if at == 0:
                    op_in[part].wait()
                    factors.append(split(op_v[rows]))
                if part == 0:
                    for copy in before_in[at]:
                        copy.wait()
                store(rows, mm3(*factors[part], dhi, dlo))
            if at == 0:
                for copy in edges_in:
                    copy.wait()
            low, high = pick(near_v[:, cols], far_v[:, cols])
            store(pl.ds(0, FACE), jnp.concatenate([low, high], axis=0))
            if last:
                made[1][:, cols] = before_v[1][:, cols] * (1.0 / center_value) + before_v[0][:, cols] + dirn_v[:, cols]
                flow.put(made[1].at[:, cols], outs[1].at[:, cols])
        flow.finish()

    return body


def change(cols, arrived, table, turned, starts, total, inner, waits):
    for p in range(SUBS):
        put_rows(inner, starts[p], arrived[p, :CAP, cols])
    usable = lax.broadcasted_iota(jnp.int32, (MID, WIDE), 0) < total
    faces = jnp.where(usable, inner[:MID], 0.0)
    pieces = jnp.concatenate([arrived[p, CAP:, cols] for p in range(SUBS)], axis=0)
    phi, plo = split(pieces)
    for copy in waits:
        copy.wait()
    both = mm(table[...], phi)
    back = both[:NPAD] + (both[NPAD:] + mm(table[:NPAD], plo))
    yhi, ylo = split(back)
    return mm(turned[...], jnp.concatenate([yhi, ylo, yhi], axis=0)), faces


def update(cols, source, edge, fix, faces, scale, store):
    rows = slice(0, FACE)
    store(rows, source[rows, cols] + scale * (edge[:, cols] - fix[rows]))
    rows = slice(FACE, FACE + MID)
    store(rows, source[rows, cols] + scale * (faces - fix[rows]))
    rows = slice(FACE + MID, LOC)
    store(rows, source[rows, cols] - scale * fix[rows])


def next_body(scale_r):
    def body(
        arrived, base, edge, table, turned, mhi, mlo, op, counts, out, near, far, dirn,
        base_v, edge_v, table_v, turned_v, mhi_v, mlo_v, ends_v, out_v, near_v, far_v, dirn_v, dhi_v, dlo_v, inner, sems,
    ):
        flow = Copies(sems)
        starts, total = face_starts(counts)
        blocks = columns(base.shape[1])
        table_in = [flow.get(table, table_v), flow.get(turned, turned_v)]
        base_in = [[flow.get(base.at[:, blocks[0]], base_v.at[:, blocks[0]]), flow.get(edge, edge_v)]]
        m_in = [flow.get(mhi, mhi_v), flow.get(mlo, mlo_v)]
        base_in += [[flow.get(base.at[:, cols], base_v.at[:, cols])] for cols in blocks[1:]]
        ends_in = flow.get(op.at[pl.ds(0, FACE)], ends_v)

        def prepare(at, cols):
            if cols is None:
                ends_in.wait()
                return
            fix, faces = change(cols, arrived, table_v, turned_v, starts, total, inner, table_in if at == 0 else ())
            for copy in base_in[at]:
                copy.wait()

            def store(rows, value):
                dirn_v[rows, cols] = value
                dhi_v[rows, cols], dlo_v[rows, cols] = split(value)

            update(cols, base_v, edge_v, fix, faces, scale_r, store)
            flow.put(dirn_v.at[:, cols], dirn.at[:, cols])
            if at == 0:
                for copy in m_in:
                    copy.wait()

        sent_rows(flow, blocks, mhi_v, mlo_v, ends_v, dhi_v, dlo_v, out, near, far, out_v, near_v, far_v, prepare)

    return body


def last_body(arrived, left, edge, table, turned, counts, res, left_v, edge_v, table_v, turned_v, res_v, inner, sems):
    flow = Copies(sems)
    starts, total = face_starts(counts)
    blocks = columns(left.shape[1])
    table_in = [flow.get(table, table_v), flow.get(turned, turned_v)]
    edge_in = flow.get(edge, edge_v)
    left_in = [flow.get(left.at[:, cols], left_v.at[:, cols]) for cols in blocks]
    for at, cols in enumerate(blocks):
        fix, faces = change(cols, arrived, table_v, turned_v, starts, total, inner, table_in if at == 0 else ())
        if at == 0:
            edge_in.wait()
        left_in[at].wait()

        def store(rows, value):
            res_v[rows, cols] = value

        update(cols, left_v, edge_v, fix, faces, 1.0, store)
        flow.put(res_v.at[:, cols], res.at[:, cols])
    flow.finish()


def pairs(first, count):
    route = []
    for low in range(first, count - 1, 2):
        route += [(low, low + 1), (low + 1, low)]
    return route


def scales():
    found, ratio = [], 1.0 / sigma_one
    for _ in range(ITERS - 1):
        ratio_next = 1.0 / (2.0 * sigma_one - ratio)
        found.append((ratio_next * ratio, 2.0 * ratio_next / half_width))
        ratio = ratio_next
    return found


def on_device(right_side, dual_operator, corner_basis, coarse_inverse, corner_map, iface_counts):
    rhs = right_side[0, 0]
    op = dual_operator[0, 0]
    basis = corner_basis[0, 0]
    inverse = coarse_inverse[0]
    counts = iface_counts[0]
    width = rhs.shape[1]
    clusters = lax.axis_size("clus")
    state, edge, sent = (LOC, width), (XC, width), (SUBS, ROWS, width)
    mids, ends = (MID + NPAD, LOC), (FACE, LOC)
    tables, turns, held = (2 * NPAD, COARSE), (LOC, 3 * NPAD), (MID + 8, WIDE)
    steps = scales()

    def exchange(out):
        return lax.all_to_all(out, "sub", split_axis=0, concat_axis=0, tiled=True)

    def swap(near, far):
        far = lax.ppermute(far, "clus", pairs(1, clusters))
        return lax.ppermute(near, "clus", pairs(0, clusters)), far

    def landed(near_in, far_in):
        return call(landed_body, (sds((FACE, width)),), (near_in, far_in), (VM, VM), (), 2, 1_000_000)[0]

    def rest(body, near, far, dirn, before, last):
        return call(
            body,
            (sds(state),) * (1 + last),
            (op, near, far, dirn) + before,
            (ANY,) * (4 + len(before)),
            (((LOC, LOC), F32), (edge, F32), (edge, F32)) + ((state, F32),) * (2 + last + len(before)),
            20,
            2_000_000_000,
        )

    out, near, far, mhi, mlo = call(
        first_body,
        (sds(sent), sds(edge), sds(edge), sds(mids, BF), sds(mids, BF)),
        (rhs, op, basis, counts),
        (ANY, ANY, ANY, SM),
        ((state, F32), ((MID + 8, LOC), F32), (ends, F32), ((NCOR, LOC), F32), (sent, F32), (edge, F32), (edge, F32), (mids, BF), (mids, BF), (state, BF), (state, BF)),
        14,
        800_000_000,
    )
    arrived = exchange(out)
    near_in, far_in = swap(near, far)
    scale_d, scale_r = steps[0]
    inverse_center = 1.0 / center_value
    made = rest(rest_body(inverse_center, scale_d * inverse_center + scale_r, None, scale_r, False), near, far, rhs, (), False)
    table, turned = call(
        table_body,
        (sds(tables, BF), sds(turns, BF)),
        (inverse, corner_map, corner_map, basis),
        (ANY, SM, ANY, ANY),
        (((COARSE, COARSE), F32), ((1, COARSE), jnp.int32), ((NCOR, LOC), F32), ((NPAD, COARSE), F32), (tables, BF), (turns, BF)),
        5,
        200_000_000,
    )
    landing = landed(near_in, far_in)
    before = (rhs,)
    for at in range(1, ITERS):
        last = at == ITERS - 1
        back_d, back_r = steps[at - 1]
        out, near, far, dirn = call(
            next_body(back_r),
            (sds(sent), sds(edge), sds(edge), sds(state)),
            (arrived, made[0], landing, table, turned, mhi, mlo, op, counts),
            (VM,) + (ANY,) * 7 + (SM,),
            ((state, F32), ((FACE, width), F32), (tables, BF), (turns, BF), (mids, BF), (mids, BF), (ends, F32), (sent, F32), (edge, F32), (edge, F32),
             (state, F32), (state, BF), (state, BF), (held, F32)),
            18,
            1_000_000_000,
        )
        arrived = exchange(out)
        near_in, far_in = swap(near, far)
        old_by = -back_d / back_r * (inverse_center if at == 1 else 1.0)
        new_by, product_by = 1.0 / back_r, 1.0
        if not last:
            scale_d, scale_r = steps[at]
            new_by, old_by, product_by = scale_d + scale_r * new_by, scale_r * old_by, scale_r
        made = rest(rest_body(1.0, new_by, old_by, product_by, last), near, far, dirn, before, last)
        landing = landed(near_in, far_in)
        before = (dirn,) + before
    (res,) = call(
        last_body,
        (sds(state),),
        (arrived, made[0], landing, table, turned, counts),
        (VM,) + (ANY,) * 4 + (SM,),
        ((state, F32), ((FACE, width), F32), (tables, BF), (turns, BF), (state, F32), (held, F32)),
        8,
        100_000_000,
    )
    return (made[1][None, None], res[None, None])


def solution(mesh):
    placed = (
        P("clus", "sub", None, None),
        P("clus", "sub", None, None),
        P("clus", "sub", None, None),
        P("clus", None, None),
        P("clus", None),
        P("clus", "sub", None),
    )
    return jax.shard_map(
        on_device,
        mesh=mesh,
        in_specs=placed,
        out_specs=(P("clus", "sub", None, None), P("clus", "sub", None, None)),
        check_vma=False,
    )
```

profile of v0, /device:TPU:96, one launch (start us, length us, event | category | flops | bytes accessed | tf_op | source)
XLA Modules:
  0.0 110.5 jit_solution(16673001269528168616)
XLA Ops:
  0.6 6.3 %shard_map.77 = (f32[16,40,512]{2,1,0:T(8,128)}, f32[128,512]{1,0:T(8,128)}, f32[128,512]{1,0:T(8,128)}, bf16[288,896]{1,0:T(8,128)(2,1)}, bf16[288,896]{1,0:T(8,128)(2,1)}) custom-call(f32[896,512]{1,0:T(8,128)} %bitcast.13, f32[896,896]{1,0:T(8,128)} %bitcast.7, f32[24,896]{1,0:T(8,128)} %bitcast.18, s32[1,16]{1,0:T(1,128)} %bitcast.20), custom_call_target="tpu_custom_call" | custom-call | flops 800000000 | bytes 6000000 | tf_op jit(solution)/shard_map/pallas_call | solution.py:53
  6.9 0.0 copy-start.7
  6.9 0.0 copy-start.5
  6.9 7.2 %all-to-all-start = ((f32[16,40,512]{2,1,0:T(8,128)}), f32[16,40,512]{2,1,0:T(8,128)S(1)}, u32[]{:S(2)}, u32[]{:S(2)}) async-start(f32[16,40,512]{2,1,0:T(8,128)} %get-tuple-element.19), calls=%async_computation | async-start | bytes 2621440 | tf_op jit(solution)/shard_map/all_to_all | solution.py:382
  14.1 0.0 copy-done.7
  14.1 0.1 collective-permute-start
  14.2 0.0 copy-done.5
  14.2 2.1 %collective-permute-start.1 = (f32[128,512]{1,0:T(8,128)S(1)}, f32[128,512]{1,0:T(8,128)S(1)}, u32[]{:S(2)}, u32[]{:S(2)}) collective-permute-start(f32[128,512]{1,0:T(8,128)S(1)} %copy-done.5), channel_id=1, source_target_pairs={{16,32},{32,16},{48,64},{64,48},{80,96},{96,80},{112,128},{128,112... | collective-permute-start | bytes 786440 | tf_op jit(solution)/shard_map/ppermute | solution.py:385
  16.3 3.1 %shard_map.80 = (bf16[64,384]{1,0:T(8,128)(2,1)}, bf16[896,96]{1,0:T(8,128)(2,1)}) custom-call(f32[384,384]{1,0:T(8,128)} %bitcast.25, s32[1,384]{1,0:T(1,128)} %place_row.1, s32[1,384]{1,0:T(1,128)} %place_row.1, f32[24,896]{1,0:T(8,128)} %bitcast.19), custom_call_target="tpu_custom_call" | custom-call | flops 200000000 | bytes 6000000 | tf_op jit(solution)/shard_map/pallas_call | solution.py:53
  19.5 6.3 %shard_map.78.base = f32[896,512]{1,0:T(8,128)} custom-call(f32[896,896]{1,0:T(8,128)} %bitcast.8, f32[128,512]{1,0:T(8,128)} %get-tuple-element.20.near, f32[128,512]{1,0:T(8,128)} %get-tuple-element.21.far, f32[896,512]{1,0:T(8,128)} %bitcast.14), custom_call_target="tpu_custom_call" | custom-call | flops 2000000000 | bytes 6000000 | tf_op jit(solution)/shard_map/pallas_call | solution.py:53
  25.8 0.0 collective-permute-done.near_in
  25.8 0.0 copy-start.10
  25.8 0.0 collective-permute-done.1.far_in
  25.8 0.7 copy-done.10
  26.5 0.0 copy-start.13
  26.5 0.7 copy-done.13
  27.2 1.9 %shard_map.79.edge = f32[256,512]{1,0:T(8,128)} custom-call(f32[128,512]{1,0:T(8,128)} %copy-done.10, f32[128,512]{1,0:T(8,128)} %copy-done.13), custom_call_target="tpu_custom_call" | custom-call | flops 1000000 | bytes 6000000 | tf_op jit(solution)/shard_map/pallas_call | solution.py:53
  29.1 5.9 %all-to-all-done.arrived = f32[16,40,512]{2,1,0:T(8,128)S(1)} async-done(((f32[16,40,512]{2,1,0:T(8,128)}), f32[16,40,512]{2,1,0:T(8,128)S(1)}, u32[]{:S(2)}, u32[]{:S(2)}) %all-to-all-start) | async-done | bytes 1310752 | tf_op jit(solution)/shard_map/all_to_all | solution.py:382
  34.9 0.0 copy-start
  34.9 1.1 copy-done
  36.0 7.3 %shard_map.81 = (f32[16,40,512]{2,1,0:T(8,128)}, f32[128,512]{1,0:T(8,128)}, f32[128,512]{1,0:T(8,128)}, f32[896,512]{1,0:T(8,128)}) custom-call(f32[16,40,512]{2,1,0:T(8,128)} %copy-done, f32[896,512]{1,0:T(8,128)} %shard_map.78.base, f32[256,512]{1,0:T(8,128)} %shard_map.79.edge, bf16[64,384]{1,0:T(8,128)(2,1)} %get-tuple-element.22.table, ...), custom_call_target="tpu_custom_call" | custom-call | flops 1000000000 | bytes 6000000 | tf_op jit(solution)/shard_map/pallas_call | solution.py:53
  43.3 0.0 copy-start.8
  43.3 0.0 copy-start.6
  43.3 3.8 %all-to-all-start.1 = ((f32[16,40,512]{2,1,0:T(8,128)}), f32[16,40,512]{2,1,0:T(8,128)S(1)}, u32[]{:S(2)}, u32[]{:S(2)}) async-start(f32[16,40,512]{2,1,0:T(8,128)} %get-tuple-element.26), calls=%async_computation.1 | async-start | bytes 2621440 | tf_op jit(solution)/shard_map/all_to_all | solution.py:382
  47.2 0.0 copy-done.8
  47.2 0.5 collective-permute-start.2
  47.7 0.0 copy-done.6
  47.7 2.1 %collective-permute-start.3 = (f32[128,512]{1,0:T(8,128)S(1)}, f32[128,512]{1,0:T(8,128)S(1)}, u32[]{:S(2)}, u32[]{:S(2)}) collective-permute-start(f32[128,512]{1,0:T(8,128)S(1)} %copy-done.6), channel_id=1, source_target_pairs={{16,32},{32,16},{48,64},{64,48},{80,96},{96,80},{112,128},{128,112... | collective-permute-start | bytes 786440 | tf_op jit(solution)/shard_map/ppermute | solution.py:385
  49.8 6.7 %shard_map.82.base = f32[896,512]{1,0:T(8,128)} custom-call(f32[896,896]{1,0:T(8,128)} %bitcast.10, f32[128,512]{1,0:T(8,128)} %get-tuple-element.27.near, f32[128,512]{1,0:T(8,128)} %get-tuple-element.28.far, f32[896,512]{1,0:T(8,128)} %get-tuple-element.29.dirn.refs_0_, f32[896,512]{1,0:T(8,128)} %bitcast.15), custom_call_target="tpu_custom_call" | custom-call | flops 2000000000 | bytes 6000000 | tf_op jit(solution)/shard_map/pallas_call | solution.py:53
  56.5 0.0 collective-permute-done.2.near_in
  56.5 0.0 copy-start.12
  56.5 0.0 collective-permute-done.3.far_in
  56.5 0.7 copy-done.12
  57.2 0.0 copy-start.14
  57.2 0.7 copy-done.14
  57.9 1.9 %shard_map.83.edge = f32[256,512]{1,0:T(8,128)} custom-call(f32[128,512]{1,0:T(8,128)} %copy-done.12, f32[128,512]{1,0:T(8,128)} %copy-done.14), custom_call_target="tpu_custom_call" | custom-call | flops 1000000 | bytes 6000000 | tf_op jit(solution)/shard_map/pallas_call | solution.py:53
  59.8 11.3 %all-to-all-done.1.arrived = f32[16,40,512]{2,1,0:T(8,128)S(1)} async-done(((f32[16,40,512]{2,1,0:T(8,128)}), f32[16,40,512]{2,1,0:T(8,128)S(1)}, u32[]{:S(2)}, u32[]{:S(2)}) %all-to-all-start.1) | async-done | bytes 1310752 | tf_op jit(solution)/shard_map/all_to_all | solution.py:382
  71.0 0.0 copy-start.1
  71.0 1.1 copy-done.1
  72.1 7.3 %shard_map.84 = (f32[16,40,512]{2,1,0:T(8,128)}, f32[128,512]{1,0:T(8,128)}, f32[128,512]{1,0:T(8,128)}, f32[896,512]{1,0:T(8,128)}) custom-call(f32[16,40,512]{2,1,0:T(8,128)} %copy-done.1, f32[896,512]{1,0:T(8,128)} %shard_map.82.base, f32[256,512]{1,0:T(8,128)} %shard_map.83.edge, bf16[64,384]{1,0:T(8,128)(2,1)} %get-tuple-element.22.table, ...), custom_call_target="tpu_custom_call" | custom-call | flops 1000000000 | bytes 6000000 | tf_op jit(solution)/shard_map/pallas_call | solution.py:53
  79.4 0.0 copy-start.4
  79.5 0.0 copy-start.3
  79.5 3.8 %all-to-all-start.2 = ((f32[16,40,512]{2,1,0:T(8,128)}), f32[16,40,512]{2,1,0:T(8,128)S(1)}, u32[]{:S(2)}, u32[]{:S(2)}) async-start(f32[16,40,512]{2,1,0:T(8,128)} %get-tuple-element.34), calls=%async_computation.2 | async-start | bytes 2621440 | tf_op jit(solution)/shard_map/all_to_all | solution.py:382
  83.3 0.0 copy-done.4
  83.3 0.1 collective-permute-start.4
  83.4 0.0 copy-done.3
  83.4 1.9 %collective-permute-start.5 = (f32[128,512]{1,0:T(8,128)S(1)}, f32[128,512]{1,0:T(8,128)S(1)}, u32[]{:S(2)}, u32[]{:S(2)}) collective-permute-start(f32[128,512]{1,0:T(8,128)S(1)} %copy-done.3), channel_id=1, source_target_pairs={{16,32},{32,16},{48,64},{64,48},{80,96},{96,80},{112,128},{128,112... | collective-permute-start | bytes 786440 | tf_op jit(solution)/shard_map/ppermute | solution.py:385
  85.4 7.5 %shard_map.85 = (f32[896,512]{1,0:T(8,128)}, f32[896,512]{1,0:T(8,128)}) custom-call(f32[896,896]{1,0:T(8,128)} %bitcast.12, f32[128,512]{1,0:T(8,128)} %get-tuple-element.30.near, f32[128,512]{1,0:T(8,128)} %get-tuple-element.31.far, f32[896,512]{1,0:T(8,128)} %get-tuple-element.32.dirn, f32[896,512]{1,0:T(8,128)} %get-tuple-element.29.dirn.refs_0_, ...), custom_call_target="tpu_custom_call" | custom-call | flops 2000000000 | bytes 6000000 | tf_op jit(solution)/shard_map/pallas_call | solution.py:53
  92.8 0.0 collective-permute-done.4.near_in
  92.9 0.0 copy-start.9
  92.9 0.0 collective-permute-done.5.far_in
  92.9 0.7 copy-done.9
  93.6 0.0 copy-start.11
  93.6 0.7 copy-done.11
  94.3 1.8 %shard_map.86.edge = f32[256,512]{1,0:T(8,128)} custom-call(f32[128,512]{1,0:T(8,128)} %copy-done.9, f32[128,512]{1,0:T(8,128)} %copy-done.11), custom_call_target="tpu_custom_call" | custom-call | flops 1000000 | bytes 6000000 | tf_op jit(solution)/shard_map/pallas_call | solution.py:53
  96.1 8.3 %all-to-all-done.2.arrived = f32[16,40,512]{2,1,0:T(8,128)S(1)} async-done(((f32[16,40,512]{2,1,0:T(8,128)}), f32[16,40,512]{2,1,0:T(8,128)S(1)}, u32[]{:S(2)}, u32[]{:S(2)}) %all-to-all-start.2) | async-done | bytes 1310752 | tf_op jit(solution)/shard_map/all_to_all | solution.py:382
  104.4 0.0 copy-start.2
  104.4 1.1 copy-done.2
  105.5 4.8 %shard_map.87 = f32[896,512]{1,0:T(8,128)} custom-call(f32[16,40,512]{2,1,0:T(8,128)} %copy-done.2, f32[896,512]{1,0:T(8,128)} %get-tuple-element.35.left, f32[256,512]{1,0:T(8,128)} %shard_map.86.edge, bf16[64,384]{1,0:T(8,128)(2,1)} %get-tuple-element.22.table, bf16[896,96]{1,0:T(8,128)(2,1)} %get-tuple-element.23.turned, s32[1,16]{1,0:T(1,128)} %bitcast.23), custom_call_target="tpu_custom_call" | custom-call | flops 100000000 | bytes 6000000 | tf_op jit(solution)/shard_map/pallas_call | solution.py:53
Async XLA Ops:
  6.9 7.2 %copy-start.7 = (f32[128,512]{1,0:T(8,128)S(1)}, f32[128,512]{1,0:T(8,128)}, u32[]{:S(2)}) copy-start(f32[128,512]{1,0:T(8,128)} %get-tuple-element.20.near) | copy-start | bytes 786436
  6.9 7.3 %copy-start.5 = (f32[128,512]{1,0:T(8,128)S(1)}, f32[128,512]{1,0:T(8,128)}, u32[]{:S(2)}) copy-start(f32[128,512]{1,0:T(8,128)} %get-tuple-element.21.far) | copy-start | bytes 786436
  6.9 28.0 %all-to-all-start = ((f32[16,40,512]{2,1,0:T(8,128)}), f32[16,40,512]{2,1,0:T(8,128)S(1)}, u32[]{:S(2)}, u32[]{:S(2)}) async-start(f32[16,40,512]{2,1,0:T(8,128)} %get-tuple-element.19), calls=%async_computation | async-start | bytes 2621440 | tf_op jit(solution)/shard_map/all_to_all | solution.py:382
  14.1 11.6 %collective-permute-start = (f32[128,512]{1,0:T(8,128)S(1)}, f32[128,512]{1,0:T(8,128)S(1)}, u32[]{:S(2)}, u32[]{:S(2)}) collective-permute-start(f32[128,512]{1,0:T(8,128)S(1)} %copy-done.7), channel_id=1, source_target_pairs={{0,16},{16,0},{32,48},{48,32},{64,80},{80,64},{96,112},{112,96},{1... | collective-permute-start | bytes 786440 | tf_op jit(solution)/shard_map/ppermute | solution.py:386
  14.2 11.5 %collective-permute-start.1 = (f32[128,512]{1,0:T(8,128)S(1)}, f32[128,512]{1,0:T(8,128)S(1)}, u32[]{:S(2)}, u32[]{:S(2)}) collective-permute-start(f32[128,512]{1,0:T(8,128)S(1)} %copy-done.5), channel_id=1, source_target_pairs={{16,32},{32,16},{48,64},{64,48},{80,96},{96,80},{112,128},{128,112... | collective-permute-start | bytes 786440 | tf_op jit(solution)/shard_map/ppermute | solution.py:385
  25.8 0.7 copy-start.10
  26.5 0.7 copy-start.13
  34.9 1.1 copy-start
  43.3 3.9 %copy-start.8 = (f32[128,512]{1,0:T(8,128)S(1)}, f32[128,512]{1,0:T(8,128)}, u32[]{:S(2)}) copy-start(f32[128,512]{1,0:T(8,128)} %get-tuple-element.27.near) | copy-start | bytes 786436
  43.3 4.4 %copy-start.6 = (f32[128,512]{1,0:T(8,128)S(1)}, f32[128,512]{1,0:T(8,128)}, u32[]{:S(2)}) copy-start(f32[128,512]{1,0:T(8,128)} %get-tuple-element.28.far) | copy-start | bytes 786436
  43.3 27.7 %all-to-all-start.1 = ((f32[16,40,512]{2,1,0:T(8,128)}), f32[16,40,512]{2,1,0:T(8,128)S(1)}, u32[]{:S(2)}, u32[]{:S(2)}) async-start(f32[16,40,512]{2,1,0:T(8,128)} %get-tuple-element.26), calls=%async_computation.1 | async-start | bytes 2621440 | tf_op jit(solution)/shard_map/all_to_all | solution.py:382
  47.2 9.3 %collective-permute-start.2 = (f32[128,512]{1,0:T(8,128)S(1)}, f32[128,512]{1,0:T(8,128)S(1)}, u32[]{:S(2)}, u32[]{:S(2)}) collective-permute-start(f32[128,512]{1,0:T(8,128)S(1)} %copy-done.8), channel_id=1, source_target_pairs={{0,16},{16,0},{32,48},{48,32},{64,80},{80,64},{96,112},{112,96},{1... | collective-permute-start | bytes 786440 | tf_op jit(solution)/shard_map/ppermute | solution.py:386
  47.7 8.8 %collective-permute-start.3 = (f32[128,512]{1,0:T(8,128)S(1)}, f32[128,512]{1,0:T(8,128)S(1)}, u32[]{:S(2)}, u32[]{:S(2)}) collective-permute-start(f32[128,512]{1,0:T(8,128)S(1)} %copy-done.6), channel_id=1, source_target_pairs={{16,32},{32,16},{48,64},{64,48},{80,96},{96,80},{112,128},{128,112... | collective-permute-start | bytes 786440 | tf_op jit(solution)/shard_map/ppermute | solution.py:385
  56.5 0.7 copy-start.12
  57.2 0.7 copy-start.14
  71.0 1.1 copy-start.1
  79.4 3.9 %copy-start.4 = (f32[128,512]{1,0:T(8,128)S(1)}, f32[128,512]{1,0:T(8,128)}, u32[]{:S(2)}) copy-start(f32[128,512]{1,0:T(8,128)} %get-tuple-element.30.near) | copy-start | bytes 786436
  79.5 4.0 %copy-start.3 = (f32[128,512]{1,0:T(8,128)S(1)}, f32[128,512]{1,0:T(8,128)}, u32[]{:S(2)}) copy-start(f32[128,512]{1,0:T(8,128)} %get-tuple-element.31.far) | copy-start | bytes 786436
  79.5 24.9 %all-to-all-start.2 = ((f32[16,40,512]{2,1,0:T(8,128)}), f32[16,40,512]{2,1,0:T(8,128)S(1)}, u32[]{:S(2)}, u32[]{:S(2)}) async-start(f32[16,40,512]{2,1,0:T(8,128)} %get-tuple-element.34), calls=%async_computation.2 | async-start | bytes 2621440 | tf_op jit(solution)/shard_map/all_to_all | solution.py:382
  83.3 9.5 %collective-permute-start.4 = (f32[128,512]{1,0:T(8,128)S(1)}, f32[128,512]{1,0:T(8,128)S(1)}, u32[]{:S(2)}, u32[]{:S(2)}) collective-permute-start(f32[128,512]{1,0:T(8,128)S(1)} %copy-done.4), channel_id=1, source_target_pairs={{0,16},{16,0},{32,48},{48,32},{64,80},{80,64},{96,112},{112,96},{1... | collective-permute-start | bytes 786440 | tf_op jit(solution)/shard_map/ppermute | solution.py:386
  83.4 9.4 %collective-permute-start.5 = (f32[128,512]{1,0:T(8,128)S(1)}, f32[128,512]{1,0:T(8,128)S(1)}, u32[]{:S(2)}, u32[]{:S(2)}) collective-permute-start(f32[128,512]{1,0:T(8,128)S(1)} %copy-done.3), channel_id=1, source_target_pairs={{16,32},{32,16},{48,64},{64,48},{80,96},{96,80},{112,128},{128,112... | collective-permute-start | bytes 786440 | tf_op jit(solution)/shard_map/ppermute | solution.py:385
  92.9 0.7 copy-start.9
  93.6 0.7 copy-start.11
  104.4 1.1 copy-start.2
where the time goes:
time: 111 us; the launch traced here: 110 us
  Pallas kernels  54.9 us (49%)
  waiting for transfers between devices  25.5 us (23%)
  starting transfers between devices  21.7 us (20%)
  local copies, waits for them, and re-layouts  7.38 us (7%)
    pallas_call x11, Pallas kernels, call(): pl.pallas_call(body, out_shape=outs, in_specs=specs, out_specs=tuple((ANY...  54.9 us
    all_to_all x3, waiting for transfers between devices, exchange(): return lax.all_to_all(out, 'sub', split_axis=0, concat_axis=0, tiled=True)  25.4 us
    all_to_all x3, starting transfers between devices, exchange(): return lax.all_to_all(out, 'sub', split_axis=0, concat_axis=0, tiled=True)  14.9 us
    unnamed x30, local copies, waits for them, and re-layouts  7.38 us
    ppermute x3, starting transfers between devices, swap(): far = lax.ppermute(far, 'clus', pairs(1, clusters))  6.11 us
  transfers between devices with their start and end apart: 9, of which 3 were waited for; matrix products, arithmetic and copies ran while one was open for 0% of the time, Pallas kernels for 26%

commit v1 on v0

--- a/solution.py
+++ b/solution.py
@@ -13,6 +13,7 @@
 CAP = 16
 SUBS = 16
 MID = SUBS * CAP
+BORDER = FACE + MID
 SPAN = CAP + 8
 ITERS = 3
 COARSE = SUBS * NCOR
@@ -25,6 +26,7 @@
 half_width = (spectrum_high - spectrum_low) / 2.0
 sigma_one = center_value / half_width
 
+WINDOW_GRANT, CRITICAL_GRANT, FIRST_GRANT = 52, 51, 59
 BF = jnp.bfloat16
 F32 = jnp.float32
 SM = pl.BlockSpec(memory_space=pltpu.SMEM)
@@ -49,14 +51,14 @@
     return jax.ShapeDtypeStruct(shape, dtype)
 
 
-def call(body, outs, ins, specs, scratch, copies, flops):
+def call(body, outs, ins, specs, scratch, copies, flops, grant=WINDOW_GRANT):
     return pl.pallas_call(
         body,
         out_shape=outs,
         in_specs=specs,
         out_specs=tuple(ANY for _ in outs),
         scratch_shapes=tuple(pltpu.VMEM(*s) for s in scratch) + (pltpu.SemaphoreType.DMA((copies,)),),
-        compiler_params=pltpu.CompilerParams(vmem_limit_bytes=56 * 1024 * 1024),
+        compiler_params=pltpu.CompilerParams(vmem_limit_bytes=grant * 1024 * 1024),
         cost_estimate=pl.CostEstimate(flops=flops, bytes_accessed=6_000_000, transcendentals=0),
     )(*ins)
 
@@ -132,28 +134,12 @@
     return jnp.where(even, far, near), jnp.where(even, near, far)
 
 
-def sent_rows(flow, blocks, mhi_v, mlo_v, ends_v, dhi_v, dlo_v, out, near, far, out_v, near_v, far_v, prepare):
-    for at, cols in enumerate(blocks):
-        prepare(at, cols)
-        fill(out_v, cols, mm3(mhi_v[...], mlo_v[...], dhi_v[:, cols], dlo_v[:, cols]))
-        flow.put(out_v.at[:, :, cols], out.at[:, :, cols])
-    prepare(len(blocks), None)
-    zhi, zlo = split(ends_v[...])
-    for cols in blocks:
-        product = mm3(zhi, zlo, dhi_v[:, cols], dlo_v[:, cols])
-        far_v[:, cols], near_v[:, cols] = pick(product[XC:], product[:XC])
-        flow.put(far_v.at[:, cols], far.at[:, cols])
-        flow.put(near_v.at[:, cols], near.at[:, cols])
-    flow.finish()
-
-
-def first_body(rhs, op, basis, counts, out, near, far, mhi, mlo, rhs_v, held, ends_v, basis_v, out_v, near_v, far_v, mhi_v, mlo_v, dhi_v, dlo_v, sems):
+def first_body(rhs, op, basis, counts, out, mhe, mle, mhr, mlr, rhs_v, held, basis_v, out_v, mhi_v, mlo_v, sems):
     flow = Copies(sems)
     rows_in = flow.get(op.at[pl.ds(FACE, MID + 8)], held)
     basis_in = flow.get(basis, basis_v)
     blocks = columns(rhs.shape[1])
     rhs_in = [flow.get(rhs.at[:, cols], rhs_v.at[:, cols]) for cols in blocks]
-    ends_in = flow.get(op.at[pl.ds(0, FACE)], ends_v)
     basis_in.wait()
     mhi_v[MID:], mlo_v[MID:] = split(padded(basis_v[...]))
     starts, _ = face_starts(counts)
@@ -161,17 +147,71 @@
     for p in range(SUBS):
         rows = slice(p * CAP, (p + 1) * CAP)
         mhi_v[rows], mlo_v[rows] = split(take_rows(held, starts[p]))
-    flow.put(mhi_v, mhi)
-    flow.put(mlo_v, mlo)
-
-    def prepare(at, cols):
-        if cols is None:
+    for cols, ready in zip(blocks, rhs_in):
+        ready.wait()
+        dhi, dlo = split(rhs_v[:, cols] * (1.0 / center_value))
+        fill(out_v, cols, mm3(mhi_v[...], mlo_v[...], dhi, dlo))
+        flow.put(out_v.at[:, :, cols], out.at[:, :, cols])
+    for source, near_face, others in ((mhi_v, mhe, mhr), (mlo_v, mle, mlr)):
+        flow.put(source.at[:, pl.ds(0, BORDER)], near_face)
+        flow.put(source.at[:, pl.ds(BORDER, LOC - BORDER)], others)
+    flow.finish()
+
+
+def edge_rows(flow, blocks, ends, direction, near, far, near_v, far_v):
+    for at, cols in enumerate(blocks):
+        dhi, dlo = split(direction(at, cols))
+        if at == 0:
+            zhi, zlo = split(ends())
+        product = mm3(zhi, zlo, dhi, dlo)
+        far_v[:, cols], near_v[:, cols] = pick(product[XC:], product[:XC])
+        flow.put(far_v.at[:, cols], far.at[:, cols])
+        flow.put(near_v.at[:, cols], near.at[:, cols])
+    flow.finish()
+
+
+def edge_first_body(rhs, op, near, far, rhs_v, ends_v, near_v, far_v, sems):
+    flow = Copies(sems)
+    blocks = columns(rhs.shape[1])
+    ends_in = flow.get(op.at[pl.ds(0, FACE)], ends_v)
+    rhs_in = [flow.get(rhs.at[:, cols], rhs_v.at[:, cols]) for cols in blocks]
+
+    def ends():
+        ends_in.wait()
+        return ends_v[...]
+
+    def direction(at, cols):
+        rhs_in[at].wait()
+        return rhs_v[:, cols] * (1.0 / center_value)
+
+    edge_rows(flow, blocks, ends, direction, near, far, near_v, far_v)
+
+
+def edge_body(scale_r):
+    def body(part, small, base, turned, op, dirn, near, far, part_v, small_v, base_v, turned_v, ends_v, dirn_v, near_v, far_v, sems):
+        flow = Copies(sems)
+        blocks = columns(base.shape[1])
+        first_in = [flow.get(turned, turned_v), flow.get(small, small_v)]
+        block_in = [[flow.get(x.at[:, cols], y.at[:, cols]) for x, y in ((part, part_v), (base.at[pl.ds(0, LOC)], base_v))] for cols in blocks]
+        ends_in = flow.get(op.at[pl.ds(0, FACE)], ends_v)
+
+        def ends():
             ends_in.wait()
-        else:
-            rhs_in[at].wait()
-            dhi_v[:, cols], dlo_v[:, cols] = split(rhs_v[:, cols] * (1.0 / center_value))
-
-    sent_rows(flow, blocks, mhi_v, mlo_v, ends_v, dhi_v, dlo_v, out, near, far, out_v, near_v, far_v, prepare)
+            return ends_v[...]
+
+        def direction(at, cols):
+            for copy in (first_in if at == 0 else []) + block_in[at]:
+                copy.wait()
+            fix = mm(turned_v[...], small_v[:, cols])
+            top, rest = slice(0, BORDER), slice(BORDER, LOC)
+            dirn_v[top, cols] = base_v[top, cols] + scale_r * (part_v[:, cols] - fix[top])
+            dirn_v[rest, cols] = base_v[rest, cols] - scale_r * fix[rest]
+            flow.put(dirn_v.at[:, cols], dirn.at[:, cols])
+            return dirn_v[:, cols]
+
+        edge_rows(flow, blocks, ends, direction, near, far, near_v, far_v)
+
+    return body
 
 
 def landed_body(near_in, far_in, edge, sems):
@@ -196,10 +236,18 @@
     return mm(top, chosen) + (mm(mid, chosen) + mm(low, chosen))
 
 
-def table_body(inverse, places, place_row, basis, table, turned, inverse_v, place_v, basis_v, rows, table_v, turned_v, sems):
+def m_copies(flow, parts, mhi_v, mlo_v):
+    mhe, mle, mhr, mlr = parts
+    top, rest = pl.ds(0, BORDER), pl.ds(BORDER, LOC - BORDER)
+    pairs_in = ((mhe, mhi_v.at[:, top]), (mhr, mhi_v.at[:, rest]), (mle, mlo_v.at[:, top]), (mlr, mlo_v.at[:, rest]))
+    return [flow.get(source, target) for source, target in pairs_in]
+
+
+def table_body(inverse, places, place_row, basis, mhe, mle, mhr, mlr, table, turned, crossed, inverse_v, place_v, basis_v, rows, mhi_v, mlo_v, table_v, turned_v, crossed_v, sems):
     flow = Copies(sems)
     inverse_in = [flow.get(inverse, inverse_v), flow.get(place_row, place_v)]
     basis_in = flow.get(basis, basis_v)
+    m_in = m_copies(flow, (mhe, mle, mhr, mlr), mhi_v, mlo_v)
     for copy in inverse_in:
         copy.wait()
     table_v[:NPAD], table_v[NPAD:] = split(table_rows(inverse_v, places, place_v, rows))
@@ -208,9 +256,15 @@
     bhi, blo = split(padded(basis_v[...]).T)
     turned_v[...] = jnp.concatenate([bhi, bhi, blo], axis=1)
     flow.put(turned_v, turned)
+    for copy in m_in:
+        copy.wait()
+    chi, clo = split(mm3(mhi_v[...], mlo_v[...], bhi, blo))
+    crossed_v[...] = jnp.concatenate([chi, chi, clo], axis=1)
+    flow.put(crossed_v, crossed)
     flow.finish()
 
 
+AHEAD = pl.ds(LOC, MID + NPAD)
 HALF = (LOC - FACE) // 2
 CHUNKS = (pl.ds(FACE, HALF), pl.ds(FACE + HALF, HALF))
 
@@ -220,12 +274,15 @@
 
     def body(op, near, far, dirn, *refs):
         before, refs = refs[:olds], refs[olds:]
+        parts, refs = (refs[:4], refs[4:]) if not last else ((), refs)
         outs, refs = refs[: 1 + last], refs[1 + last :]
         (op_v, near_v, far_v, dirn_v), refs = refs[:4], refs[4:]
-        before_v, made, sems = refs[:olds], refs[olds:-1], refs[-1]
+        before_v, refs = refs[:olds], refs[olds:]
+        m_v, refs = (refs[:2], refs[2:]) if not last else ((), refs)
+        made, sems = refs[:-1], refs[-1]
         flow = Copies(sems)
         blocks = columns(dirn.shape[1])
-        op_in, dirn_in, before_in = [], [], []
+        op_in, dirn_in, before_in, m_in = [], [], [], []
         for at, cols in enumerate(blocks):
             dirn_in.append(flow.get(dirn.at[:, cols], dirn_v.at[:, cols]))
             if at == 0:
@@ -234,6 +291,7 @@
             if at == 0:
                 op_in.append(flow.get(op.at[CHUNKS[1]], op_v.at[CHUNKS[1]]))
                 edges_in = [flow.get(near, near_v), flow.get(far, far_v)]
+                m_in = [] if last else m_copies(flow, parts, *m_v)
         factors = []
         for at, cols in enumerate(blocks):
             dirn_in[at].wait()
@@ -262,24 +320,31 @@
             if last:
                 made[1][:, cols] = before_v[1][:, cols] * (1.0 / center_value) + before_v[0][:, cols] + dirn_v[:, cols]
                 flow.put(made[1].at[:, cols], outs[1].at[:, cols])
+            else:
+                if at == 0:
+                    for copy in m_in:
+                        copy.wait()
+                made[1][:, cols] = mm3(m_v[0][...], m_v[1][...], *split(made[0][:, cols]))
+                flow.put(made[1].at[:, cols], outs[0].at[AHEAD, cols])
         flow.finish()
 
     return body
 
 
-def change(cols, arrived, table, turned, starts, total, inner, waits):
+def arrived_faces(cols, arrived, starts, total, inner):
     for p in range(SUBS):
         put_rows(inner, starts[p], arrived[p, :CAP, cols])
     usable = lax.broadcasted_iota(jnp.int32, (MID, WIDE), 0) < total
-    faces = jnp.where(usable, inner[:MID], 0.0)
+    return jnp.where(usable, inner[:MID], 0.0)
+
+
+def arrived_back(cols, arrived, table):
     pieces = jnp.concatenate([arrived[p, CAP:, cols] for p in range(SUBS)], axis=0)
     phi, plo = split(pieces)
-    for copy in waits:
-        copy.wait()
     both = mm(table[...], phi)
     back = both[:NPAD] + (both[NPAD:] + mm(table[:NPAD], plo))
     yhi, ylo = split(back)
-    return mm(turned[...], jnp.concatenate([yhi, ylo, yhi], axis=0)), faces
+    return jnp.concatenate([yhi, ylo, yhi], axis=0)
 
 
 def update(cols, source, edge, fix, faces, scale, store):
@@ -292,38 +357,26 @@
 
 
 def next_body(scale_r):
-    def body(
-        arrived, base, edge, table, turned, mhi, mlo, op, counts, out, near, far, dirn,
-        base_v, edge_v, table_v, turned_v, mhi_v, mlo_v, ends_v, out_v, near_v, far_v, dirn_v, dhi_v, dlo_v, inner, sems,
-    ):
+    def body(arrived, mhe, mle, table, crossed, ahead, edge, counts, out, part, small, ahead_v, part_v, small_v, out_v, inner, sems):
         flow = Copies(sems)
+        edge_in = flow.get(edge, part_v.at[pl.ds(0, FACE)])
+        ahead_in = flow.get(ahead.at[AHEAD], ahead_v)
         starts, total = face_starts(counts)
-        blocks = columns(base.shape[1])
-        table_in = [flow.get(table, table_v), flow.get(turned, turned_v)]
-        base_in = [[flow.get(base.at[:, blocks[0]], base_v.at[:, blocks[0]]), flow.get(edge, edge_v)]]
-        m_in = [flow.get(mhi, mhi_v), flow.get(mlo, mlo_v)]
-        base_in += [[flow.get(base.at[:, cols], base_v.at[:, cols])] for cols in blocks[1:]]
-        ends_in = flow.get(op.at[pl.ds(0, FACE)], ends_v)
-
-        def prepare(at, cols):
-            if cols is None:
-                ends_in.wait()
-                return
-            fix, faces = change(cols, arrived, table_v, turned_v, starts, total, inner, table_in if at == 0 else ())
-            for copy in base_in[at]:
-                copy.wait()
-
-            def store(rows, value):
-                dirn_v[rows, cols] = value
-                dhi_v[rows, cols], dlo_v[rows, cols] = split(value)
-
-            update(cols, base_v, edge_v, fix, faces, scale_r, store)
-            flow.put(dirn_v.at[:, cols], dirn.at[:, cols])
+        blocks = columns(edge.shape[1])
+        for at, cols in enumerate(blocks):
+            back = arrived_back(cols, arrived, table)
+            small_v[:, cols] = back
+            part_v[FACE:, cols] = arrived_faces(cols, arrived, starts, total, inner)
             if at == 0:
-                for copy in m_in:
-                    copy.wait()
-
-        sent_rows(flow, blocks, mhi_v, mlo_v, ends_v, dhi_v, dlo_v, out, near, far, out_v, near_v, far_v, prepare)
+                edge_in.wait()
+            product = mm3(mhe[...], mle[...], *split(part_v[:, cols])) - mm(crossed[...], back)
+            if at == 0:
+                ahead_in.wait()
+            fill(out_v, cols, ahead_v[:, cols] + scale_r * product)
+            flow.put(out_v.at[:, :, cols], out.at[:, :, cols])
+            flow.put(part_v.at[:, cols], part.at[:, cols])
+        flow.put(small_v, small)
+        flow.finish()
 
     return body
 
@@ -336,7 +389,11 @@
     edge_in = flow.get(edge, edge_v)
     left_in = [flow.get(left.at[:, cols], left_v.at[:, cols]) for cols in blocks]
     for at, cols in enumerate(blocks):
-        fix, faces = change(cols, arrived, table_v, turned_v, starts, total, inner, table_in if at == 0 else ())
+        faces = arrived_faces(cols, arrived, starts, total, inner)
+        if at == 0:
+            for copy in table_in:
+                copy.wait()
+        fix = mm(turned_v[...], arrived_back(cols, arrived, table_v))
         if at == 0:
             edge_in.wait()
         left_in[at].wait()
@@ -386,58 +443,86 @@
         return lax.ppermute(near, "clus", pairs(0, clusters)), far
 
     def landed(near_in, far_in):
-        return call(landed_body, (sds((FACE, width)),), (near_in, far_in), (VM, VM), (), 2, 1_000_000)[0]
+        return call(landed_body, (sds((FACE, width)),), (near_in, far_in), (VM, VM), (), 2, 1_000_000, WINDOW_GRANT)[0]
+
+    border, others = (MID + NPAD, BORDER), (MID + NPAD, LOC - BORDER)
+    crosses, ahead_s, part_s, small_s = (MID + NPAD, 3 * NPAD), (MID + NPAD, width), (BORDER, width), (3 * NPAD, width)
+    inverse_center = 1.0 / center_value
+
+    out, mhe, mle, mhr, mlr = call(
+        first_body,
+        (sds(sent), sds(border, BF), sds(border, BF), sds(others, BF), sds(others, BF)),
+        (rhs, op, basis, counts),
+        (ANY, ANY, ANY, SM),
+        ((state, F32), ((MID + 8, LOC), F32), ((NCOR, LOC), F32), (sent, F32), (mids, BF), (mids, BF)),
+        10,
+        800_000_000,
+        FIRST_GRANT,
+    )
+    parts = (mhe, mle, mhr, mlr)
 
     def rest(body, near, far, dirn, before, last):
         return call(
             body,
-            (sds(state),) * (1 + last),
-            (op, near, far, dirn) + before,
-            (ANY,) * (4 + len(before)),
-            (((LOC, LOC), F32), (edge, F32), (edge, F32)) + ((state, F32),) * (2 + last + len(before)),
-            20,
+            (sds(state), sds(state)) if last else (sds((LOC + MID + NPAD, width)),),
+            (op, near, far, dirn) + before + (() if last else parts),
+            (ANY,) * (4 + len(before) + 4 * (not last)),
+            (((LOC, LOC), F32), (edge, F32), (edge, F32), (state, F32)) + ((state, F32),) * len(before)
+            + (() if last else ((mids, BF), (mids, BF))) + ((state, F32), (state if last else ahead_s, F32)),
+            24,
             2_000_000_000,
+            WINDOW_GRANT,
         )
 
-    out, near, far, mhi, mlo = call(
-        first_body,
-        (sds(sent), sds(edge), sds(edge), sds(mids, BF), sds(mids, BF)),
-        (rhs, op, basis, counts),
-        (ANY, ANY, ANY, SM),
-        ((state, F32), ((MID + 8, LOC), F32), (ends, F32), ((NCOR, LOC), F32), (sent, F32), (edge, F32), (edge, F32), (mids, BF), (mids, BF), (state, BF), (state, BF)),
-        14,
-        800_000_000,
+    arrived = exchange(out)
+    near, far = call(
+        edge_first_body,
+        (sds(edge), sds(edge)),
+        (rhs, op),
+        (ANY, ANY),
+        ((state, F32), (ends, F32), (edge, F32), (edge, F32)),
+        7,
+        700_000_000,
     )
-    arrived = exchange(out)
     near_in, far_in = swap(near, far)
     scale_d, scale_r = steps[0]
-    inverse_center = 1.0 / center_value
     made = rest(rest_body(inverse_center, scale_d * inverse_center + scale_r, None, scale_r, False), near, far, rhs, (), False)
-    table, turned = call(
+    table, turned, crossed = call(
         table_body,
-        (sds(tables, BF), sds(turns, BF)),
-        (inverse, corner_map, corner_map, basis),
-        (ANY, SM, ANY, ANY),
-        (((COARSE, COARSE), F32), ((1, COARSE), jnp.int32), ((NCOR, LOC), F32), ((NPAD, COARSE), F32), (tables, BF), (turns, BF)),
-        5,
+        (sds(tables, BF), sds(turns, BF), sds(crosses, BF)),
+        (inverse, corner_map, corner_map, basis) + parts,
+        (ANY, SM) + (ANY,) * 6,
+        (((COARSE, COARSE), F32), ((1, COARSE), jnp.int32), ((NCOR, LOC), F32), ((NPAD, COARSE), F32), (mids, BF), (mids, BF),
+         (tables, BF), (turns, BF), (crosses, BF)),
+        10,
         200_000_000,
+        WINDOW_GRANT,
     )
     landing = landed(near_in, far_in)
     before = (rhs,)
     for at in range(1, ITERS):
         last = at == ITERS - 1
         back_d, back_r = steps[at - 1]
-        out, near, far, dirn = call(
+        out, part, small = call(
             next_body(back_r),
-            (sds(sent), sds(edge), sds(edge), sds(state)),
-            (arrived, made[0], landing, table, turned, mhi, mlo, op, counts),
-            (VM,) + (ANY,) * 7 + (SM,),
-            ((state, F32), ((FACE, width), F32), (tables, BF), (turns, BF), (mids, BF), (mids, BF), (ends, F32), (sent, F32), (edge, F32), (edge, F32),
-             (state, F32), (state, BF), (state, BF), (held, F32)),
-            18,
+            (sds(sent), sds(part_s), sds(small_s, BF)),
+            (arrived, mhe, mle, table, crossed, made[0], landing, counts),
+            (VM,) * 5 + (ANY,) * 2 + (SM,),
+            ((ahead_s, F32), (part_s, F32), (small_s, BF), (sent, F32), (held, F32)),
+            7,
             1_000_000_000,
+            CRITICAL_GRANT,
         )
         arrived = exchange(out)
+        dirn, near, far = call(
+            edge_body(back_r),
+            (sds(state), sds(edge), sds(edge)),
+            (part, small, made[0], turned, op),
+            (ANY,) * 5,
+            ((part_s, F32), (small_s, BF), (state, F32), (turns, BF), (ends, F32), (state, F32), (edge, F32), (edge, F32)),
+            13,
+            700_000_000,
+        )
         near_in, far_in = swap(near, far)
         old_by = -back_d / back_r * (inverse_center if at == 1 else 1.0)
         new_by, product_by = 1.0 / back_r, 1.0
@@ -455,6 +540,7 @@
         ((state, F32), ((FACE, width), F32), (tables, BF), (turns, BF), (state, F32), (held, F32)),
         8,
         100_000_000,
+        CRITICAL_GRANT,
     )
     return (made[1][None, None], res[None, None])
 

time: 111 us -> 103 us (0.928); the launches traced: 110 us -> 101 us
  waiting for transfers between devices: 25.5 us -> 11.7 us
  local copies, waits for them, and re-layouts: 7.38 us -> 0.04 us
  starting transfers between devices: 21.7 us -> 28.6 us
  Pallas kernels: 54.9 us -> 59.8 us
    all_to_all x3, waiting for transfers between devices: 25.4 us -> 11.7 us  [exchange(): return lax.all_to_all(out, 'sub', split_axis=0, concat_axis=0, tiled=True)]
    unnamed x30 -> x14, local copies, waits for them, and re-layouts: 7.38 us -> 0.04 us
    pallas_call x11 -> x14, Pallas kernels: 54.9 us -> 59.8 us  [call(): pl.pallas_call(body, out_shape=outs, in_specs=specs, out_specs=tuple((ANY...]
    ppermute x3, starting transfers between devices: 0.68 us -> 3.61 us  [swap(): return (lax.ppermute(near, 'clus', pairs(0, clusters)), far)]
    all_to_all x3, starting transfers between devices: 14.9 us -> 17.1 us  [exchange(): return lax.all_to_all(out, 'sub', split_axis=0, concat_axis=0, tiled=True)]
    ppermute x3, starting transfers between devices: 6.11 us -> 7.82 us  [swap(): far = lax.ppermute(far, 'clus', pairs(1, clusters))]
  transfers between devices with their start and end apart: 9 -> 9, of which waited for: 3 -> 3; matrix products, arithmetic and copies ran while one was open for 0% -> 0% of each run, Pallas kernels for 26% -> 41%
where the time goes in v1:
time: 103 us; the launch traced here: 101 us
  Pallas kernels  59.8 us (58%)
  starting transfers between devices  28.6 us (28%)
  waiting for transfers between devices  11.7 us (11%)
  between operations  1.12 us (1%)
    pallas_call x14, Pallas kernels, call(): pl.pallas_call(body, out_shape=outs, in_specs=specs, out_specs=tuple((ANY...  59.8 us
    all_to_all x3, starting transfers between devices, exchange(): return lax.all_to_all(out, 'sub', split_axis=0, concat_axis=0, tiled=True)  17.1 us
    all_to_all x3, waiting for transfers between devices, exchange(): return lax.all_to_all(out, 'sub', split_axis=0, concat_axis=0, tiled=True)  11.7 us
    ppermute x3, starting transfers between devices, swap(): far = lax.ppermute(far, 'clus', pairs(1, clusters))  7.82 us
    ppermute x3, starting transfers between devices, swap(): return (lax.ppermute(near, 'clus', pairs(0, clusters)), far)  3.61 us
  transfers between devices with their start and end apart: 9, of which 3 were waited for; matrix products, arithmetic and copies ran while one was open for 0% of the time, Pallas kernels for 41%

profile of v1, /device:TPU:96, one launch (start us, length us, event | category | flops | bytes accessed | tf_op | source)
XLA Modules:
  0.0 101.3 jit_solution(14981981169481236456)
XLA Ops:
  0.6 5.6 %shard_map.77 = (f32[16,40,512]{2,1,0:T(8,128)}, bf16[288,512]{1,0:T(8,128)(2,1)}, bf16[288,512]{1,0:T(8,128)(2,1)}, bf16[288,384]{1,0:T(8,128)(2,1)}, bf16[288,384]{1,0:T(8,128)(2,1)}) custom-call(f32[896,512]{1,0:T(8,128)} %bitcast.20, f32[896,896]{1,0:T(8,128)} %bitcast.13, f32[24,896]{1,0:T(8,128)} %bitcast.7, s32[1,16]{1,0:T(1,128)} %bitcast.9), custom_call_target="tpu_custom_call" | custom-call | flops 800000000 | bytes 6000000 | tf_op jit(solution)/shard_map/pallas_call | solution.py:55
  6.2 7.1 %all-to-all-start = ((f32[16,40,512]{2,1,0:T(8,128)}), f32[16,40,512]{2,1,0:T(8,128)}, u32[]{:S(2)}, u32[]{:S(2)}) async-start(f32[16,40,512]{2,1,0:T(8,128)} %get-tuple-element.26), calls=%async_computation | async-start | bytes 2621440 | tf_op jit(solution)/shard_map/all_to_all | solution.py:439
  13.3 0.0 copy-start
  13.3 0.0 copy-start.1
  13.4 0.0 copy-start.2
  13.4 0.0 copy-start.3
  13.4 0.0 copy-start.4
  13.4 0.0 copy-start.6
  13.4 3.8 %shard_map.79 = (f32[128,512]{1,0:T(8,128)S(1)}, f32[128,512]{1,0:T(8,128)S(1)}) custom-call(f32[896,512]{1,0:T(8,128)} %bitcast.21, f32[896,896]{1,0:T(8,128)} %bitcast.14), custom_call_target="tpu_custom_call" | custom-call | flops 700000000 | bytes 6000000 | tf_op jit(solution)/shard_map/pallas_call | solution.py:55
  17.2 0.1 collective-permute-start
  17.3 2.1 %collective-permute-start.1 = (f32[128,512]{1,0:T(8,128)S(1)}, f32[128,512]{1,0:T(8,128)S(1)}, u32[]{:S(2)}, u32[]{:S(2)}) collective-permute-start(f32[128,512]{1,0:T(8,128)S(1)} %get-tuple-element.34.far), channel_id=1, source_target_pairs={{16,32},{32,16},{48,64},{64,48},{80,96},{96,80},{112,128},{128,112... | collective-permute-start | bytes 786440 | tf_op jit(solution)/shard_map/ppermute | solution.py:442
  19.4 0.0 copy-done
  19.4 0.0 copy-done.1
  19.4 0.0 copy-done.2
  19.4 0.0 copy-done.3
  19.4 0.0 copy-done.4
  19.4 0.0 copy-done.6
  19.5 3.5 %shard_map.78 = (bf16[64,384]{1,0:T(8,128)(2,1)S(1)}, bf16[896,96]{1,0:T(8,128)(2,1)S(1)}, bf16[288,96]{1,0:T(8,128)(2,1)S(1)}) custom-call(f32[384,384]{1,0:T(8,128)} %bitcast.26, s32[1,384]{1,0:T(1,128)S(1)} %copy-done.6, s32[1,384]{1,0:T(1,128)S(1)} %copy-done.6, f32[24,896]{1,0:T(8,128)S(1)} %bitcast.8, bf16[288,512]{1,0:T(8,128)(2,1)S(1)} %copy-done, ...), custom_call_target="tpu_custom_call" | custom-call | flops 200000000 | bytes 6000000 | tf_op jit(solution)/shard_map/pallas_call | solution.py:55
  22.9 0.0 copy-start.5
  23.0 8.2 %shard_map.80.ahead.base = f32[1184,512]{1,0:T(8,128)} custom-call(f32[896,896]{1,0:T(8,128)} %bitcast.15, f32[128,512]{1,0:T(8,128)S(1)} %get-tuple-element.33.near, f32[128,512]{1,0:T(8,128)S(1)} %get-tuple-element.34.far, f32[896,512]{1,0:T(8,128)} %bitcast.22, bf16[288,512]{1,0:T(8,128)(2,1)S(1)} %copy-done, bf16[288,512]{1,0:T(8,128)(2,1)S(1)} %copy-done.1, ...), custom_call_target="tpu_custom_call" | custom-call | flops 2000000000 | bytes 6000000 | tf_op jit(solution)/shard_map/pallas_call | solution.py:55
  31.2 0.0 collective-permute-done.near_in
  31.2 0.0 collective-permute-done.1.far_in
  31.2 0.1 shard_map.81.edge
  31.3 2.9 %all-to-all-done.arrived = f32[16,40,512]{2,1,0:T(8,128)} async-done(((f32[16,40,512]{2,1,0:T(8,128)}), f32[16,40,512]{2,1,0:T(8,128)}, u32[]{:S(2)}, u32[]{:S(2)}) %all-to-all-start) | async-done | bytes 1310752 | tf_op jit(solution)/shard_map/all_to_all | solution.py:439
  34.2 0.0 copy-done.5
  34.2 4.4 %shard_map.82 = (f32[16,40,512]{2,1,0:T(8,128)}, f32[512,512]{1,0:T(8,128)S(1)}, bf16[96,512]{1,0:T(8,128)(2,1)S(1)}) custom-call(f32[16,40,512]{2,1,0:T(8,128)} %all-to-all-done.arrived, bf16[288,512]{1,0:T(8,128)(2,1)S(1)} %copy-done, bf16[288,512]{1,0:T(8,128)(2,1)S(1)} %copy-done.1, bf16[64,384]{1,0:T(8,128)(2,1)S(1)} %get-tuple-element.31.table, ...), custom_call_target="tpu_custom_call" | custom-call | flops 1000000000 | bytes 6000000 | tf_op jit(solution)/shard_map/pallas_call | solution.py:55
  38.6 4.6 %all-to-all-start.1 = ((f32[16,40,512]{2,1,0:T(8,128)}), f32[16,40,512]{2,1,0:T(8,128)}, u32[]{:S(2)}, u32[]{:S(2)}) async-start(f32[16,40,512]{2,1,0:T(8,128)} %get-tuple-element.35), calls=%async_computation.1 | async-start | bytes 2621440 | tf_op jit(solution)/shard_map/all_to_all | solution.py:439
  43.2 4.6 %shard_map.83 = (f32[896,512]{1,0:T(8,128)}, f32[128,512]{1,0:T(8,128)S(1)}, f32[128,512]{1,0:T(8,128)S(1)}) custom-call(f32[512,512]{1,0:T(8,128)S(1)} %get-tuple-element.36.part, bf16[96,512]{1,0:T(8,128)(2,1)S(1)} %get-tuple-element.37.small, f32[1184,512]{1,0:T(8,128)} %shard_map.80.ahead.base, bf16[896,96]{1,0:T(8,128)(2,1)S(1)} %get-tuple-element.38.turned, ...), custom_call_target="tpu_custom_call" | custom-call | flops 700000000 | bytes 6000000 | tf_op jit(solution)/shard_map/pallas_call | solution.py:55
  47.9 2.6 %collective-permute-start.2 = (f32[128,512]{1,0:T(8,128)S(1)}, f32[128,512]{1,0:T(8,128)S(1)}, u32[]{:S(2)}, u32[]{:S(2)}) collective-permute-start(f32[128,512]{1,0:T(8,128)S(1)} %get-tuple-element.39.near), channel_id=1, source_target_pairs={{0,16},{16,0},{32,48},{48,32},{64,80},{80,64},{96,112},{112,96},{1... | collective-permute-start | bytes 786440 | tf_op jit(solution)/shard_map/ppermute | solution.py:443
  50.5 1.9 %collective-permute-start.3 = (f32[128,512]{1,0:T(8,128)S(1)}, f32[128,512]{1,0:T(8,128)S(1)}, u32[]{:S(2)}, u32[]{:S(2)}) collective-permute-start(f32[128,512]{1,0:T(8,128)S(1)} %get-tuple-element.40.far), channel_id=1, source_target_pairs={{16,32},{32,16},{48,64},{64,48},{80,96},{96,80},{112,128},{128,112... | collective-permute-start | bytes 786440 | tf_op jit(solution)/shard_map/ppermute | solution.py:442
  52.4 8.7 %shard_map.84.ahead.base = f32[1184,512]{1,0:T(8,128)} custom-call(f32[896,896]{1,0:T(8,128)} %bitcast.17, f32[128,512]{1,0:T(8,128)S(1)} %get-tuple-element.39.near, f32[128,512]{1,0:T(8,128)S(1)} %get-tuple-element.40.far, f32[896,512]{1,0:T(8,128)} %get-tuple-element.41.dirn.refs_0_, f32[896,512]{1,0:T(8,128)} %bitcast.23, bf16[288,512]{1,0:T(8,128)(2,1)S(1)} %copy-done, ...), custom_call_target="tpu_custom_call" | custom-call | flops 2000000000 | bytes 6000000 | tf_op jit(solution)/shard_map/pallas_call | solution.py:55
  61.1 0.0 collective-permute-done.2.near_in
  61.1 0.0 collective-permute-done.3.far_in
  61.1 0.1 shard_map.85.edge
  61.2 1.4 %all-to-all-done.1.arrived = f32[16,40,512]{2,1,0:T(8,128)} async-done(((f32[16,40,512]{2,1,0:T(8,128)}), f32[16,40,512]{2,1,0:T(8,128)}, u32[]{:S(2)}, u32[]{:S(2)}) %all-to-all-start.1) | async-done | bytes 1310752 | tf_op jit(solution)/shard_map/all_to_all | solution.py:439
  62.7 4.5 %shard_map.86 = (f32[16,40,512]{2,1,0:T(8,128)}, f32[512,512]{1,0:T(8,128)S(1)}, bf16[96,512]{1,0:T(8,128)(2,1)S(1)}) custom-call(f32[16,40,512]{2,1,0:T(8,128)} %all-to-all-done.1.arrived, bf16[288,512]{1,0:T(8,128)(2,1)S(1)} %copy-done, bf16[288,512]{1,0:T(8,128)(2,1)S(1)} %copy-done.1, bf16[64,384]{1,0:T(8,128)(2,1)S(1)} %get-tuple-element.31.table, ...), custom_call_target="tpu_custom_call" | custom-call | flops 1000000000 | bytes 6000000 | tf_op jit(solution)/shard_map/pallas_call | solution.py:55
  67.2 5.5 %all-to-all-start.2 = ((f32[16,40,512]{2,1,0:T(8,128)}), f32[16,40,512]{2,1,0:T(8,128)S(1)}, u32[]{:S(2)}, u32[]{:S(2)}) async-start(f32[16,40,512]{2,1,0:T(8,128)} %get-tuple-element.48), calls=%async_computation.2 | async-start | bytes 2621440 | tf_op jit(solution)/shard_map/all_to_all | solution.py:439
  72.6 4.7 %shard_map.87 = (f32[896,512]{1,0:T(8,128)}, f32[128,512]{1,0:T(8,128)S(1)}, f32[128,512]{1,0:T(8,128)S(1)}) custom-call(f32[512,512]{1,0:T(8,128)S(1)} %get-tuple-element.42.part, bf16[96,512]{1,0:T(8,128)(2,1)S(1)} %get-tuple-element.43.small, f32[1184,512]{1,0:T(8,128)} %shard_map.84.ahead.base, bf16[896,96]{1,0:T(8,128)(2,1)S(1)} %get-tuple-element.38.turned, ...), custom_call_target="tpu_custom_call" | custom-call | flops 700000000 | bytes 6000000 | tf_op jit(solution)/shard_map/pallas_call | solution.py:55
  77.3 0.9 collective-permute-start.4
  78.2 3.8 %collective-permute-start.5 = (f32[128,512]{1,0:T(8,128)S(1)}, f32[128,512]{1,0:T(8,128)S(1)}, u32[]{:S(2)}, u32[]{:S(2)}) collective-permute-start(f32[128,512]{1,0:T(8,128)S(1)} %get-tuple-element.45.far), channel_id=1, source_target_pairs={{16,32},{32,16},{48,64},{64,48},{80,96},{96,80},{112,128},{128,112... | collective-permute-start | bytes 786440 | tf_op jit(solution)/shard_map/ppermute | solution.py:442
  82.0 7.5 %shard_map.88 = (f32[896,512]{1,0:T(8,128)}, f32[896,512]{1,0:T(8,128)}) custom-call(f32[896,896]{1,0:T(8,128)} %bitcast.19, f32[128,512]{1,0:T(8,128)S(1)} %get-tuple-element.44.near, f32[128,512]{1,0:T(8,128)S(1)} %get-tuple-element.45.far, f32[896,512]{1,0:T(8,128)} %get-tuple-element.46.dirn, f32[896,512]{1,0:T(8,128)} %get-tuple-element.41.dirn.refs_0_, ...), custom_call_target="tpu_custom_call" | custom-call | flops 2000000000 | bytes 6000000 | tf_op jit(solution)/shard_map/pallas_call | solution.py:55
  89.6 0.0 collective-permute-done.4.near_in
  89.6 0.0 collective-permute-done.5.far_in
  89.6 0.1 shard_map.89.edge
  89.7 7.3 %all-to-all-done.2.arrived = f32[16,40,512]{2,1,0:T(8,128)S(1)} async-done(((f32[16,40,512]{2,1,0:T(8,128)}), f32[16,40,512]{2,1,0:T(8,128)S(1)}, u32[]{:S(2)}, u32[]{:S(2)}) %all-to-all-start.2) | async-done | bytes 1310752 | tf_op jit(solution)/shard_map/all_to_all | solution.py:439
  97.0 4.1 %shard_map.90 = f32[896,512]{1,0:T(8,128)} custom-call(f32[16,40,512]{2,1,0:T(8,128)S(1)} %all-to-all-done.2.arrived, f32[896,512]{1,0:T(8,128)} %get-tuple-element.49.left, f32[256,512]{1,0:T(8,128)S(1)} %shard_map.89.edge, bf16[64,384]{1,0:T(8,128)(2,1)S(1)} %get-tuple-element.31.table, bf16[896,96]{1,0:T(8,128)(2,1)S(1)} %get-tuple-element.38.turned, ...), custom_call_target="tpu_custom_call" | custom-call | flops 100000000 | bytes 6000000 | tf_op jit(solution)/shard_map/pallas_call | solution.py:55
Async XLA Ops:
  6.2 28.0 %all-to-all-start = ((f32[16,40,512]{2,1,0:T(8,128)}), f32[16,40,512]{2,1,0:T(8,128)}, u32[]{:S(2)}, u32[]{:S(2)}) async-start(f32[16,40,512]{2,1,0:T(8,128)} %get-tuple-element.26), calls=%async_computation | async-start | bytes 2621440 | tf_op jit(solution)/shard_map/all_to_all | solution.py:439
  13.3 6.1 %copy-start = (bf16[288,512]{1,0:T(8,128)(2,1)S(1)}, bf16[288,512]{1,0:T(8,128)(2,1)}, u32[]{:S(2)}) copy-start(bf16[288,512]{1,0:T(8,128)(2,1)} %get-tuple-element.27.mhe.refs_0_.refs_1_) | copy-start | bytes 884740
  13.3 6.1 %copy-start.1 = (bf16[288,512]{1,0:T(8,128)(2,1)S(1)}, bf16[288,512]{1,0:T(8,128)(2,1)}, u32[]{:S(2)}) copy-start(bf16[288,512]{1,0:T(8,128)(2,1)} %get-tuple-element.28.mle.refs_1_.refs_2_) | copy-start | bytes 884740
  13.4 6.1 %copy-start.2 = (bf16[288,384]{1,0:T(8,128)(2,1)S(1)}, bf16[288,384]{1,0:T(8,128)(2,1)}, u32[]{:S(2)}) copy-start(bf16[288,384]{1,0:T(8,128)(2,1)} %get-tuple-element.29.mhr.refs_2_.refs_3_) | copy-start | bytes 663556
  13.4 6.1 %copy-start.3 = (bf16[288,384]{1,0:T(8,128)(2,1)S(1)}, bf16[288,384]{1,0:T(8,128)(2,1)}, u32[]{:S(2)}) copy-start(bf16[288,384]{1,0:T(8,128)(2,1)} %get-tuple-element.30.mlr.refs_3_.refs_4_) | copy-start | bytes 663556
  13.4 6.1 %copy-start.4 = (f32[1,1,24,896]{3,2,1,0:T(8,128)S(1)}, f32[1,1,24,896]{3,2,1,0:T(8,128)}, u32[]{:S(2)}) copy-start(f32[1,1,24,896]{3,2,1,0:T(8,128)} %param.8) | copy-start | bytes 258052
  13.4 6.1 %copy-start.6 = (s32[1,384]{1,0:T(1,128)S(1)}, s32[1,384]{1,0:T(1,128)}, u32[]{:S(2)}) copy-start(s32[1,384]{1,0:T(1,128)} %place_row.1) | copy-start | bytes 4612
  17.2 14.0 %collective-permute-start = (f32[128,512]{1,0:T(8,128)S(1)}, f32[128,512]{1,0:T(8,128)S(1)}, u32[]{:S(2)}, u32[]{:S(2)}) collective-permute-start(f32[128,512]{1,0:T(8,128)S(1)} %get-tuple-element.33.near), channel_id=1, source_target_pairs={{0,16},{16,0},{32,48},{48,32},{64,80},{80,64},{96,112},{112,96},{1... | collective-permute-start | bytes 786440 | tf_op jit(solution)/shard_map/ppermute | solution.py:443
  17.3 13.9 %collective-permute-start.1 = (f32[128,512]{1,0:T(8,128)S(1)}, f32[128,512]{1,0:T(8,128)S(1)}, u32[]{:S(2)}, u32[]{:S(2)}) collective-permute-start(f32[128,512]{1,0:T(8,128)S(1)} %get-tuple-element.34.far), channel_id=1, source_target_pairs={{16,32},{32,16},{48,64},{64,48},{80,96},{96,80},{112,128},{128,112... | collective-permute-start | bytes 786440 | tf_op jit(solution)/shard_map/ppermute | solution.py:442
  22.9 11.3 %copy-start.5 = (s32[1,1,16]{2,1,0:T(1,128)S(1)}, s32[1,1,16]{2,1,0:T(1,128)}, u32[]{:S(2)}) copy-start(s32[1,1,16]{2,1,0:T(1,128)} %param.11) | copy-start | bytes 196
  38.6 24.0 %all-to-all-start.1 = ((f32[16,40,512]{2,1,0:T(8,128)}), f32[16,40,512]{2,1,0:T(8,128)}, u32[]{:S(2)}, u32[]{:S(2)}) async-start(f32[16,40,512]{2,1,0:T(8,128)} %get-tuple-element.35), calls=%async_computation.1 | async-start | bytes 2621440 | tf_op jit(solution)/shard_map/all_to_all | solution.py:439
  47.9 13.2 %collective-permute-start.2 = (f32[128,512]{1,0:T(8,128)S(1)}, f32[128,512]{1,0:T(8,128)S(1)}, u32[]{:S(2)}, u32[]{:S(2)}) collective-permute-start(f32[128,512]{1,0:T(8,128)S(1)} %get-tuple-element.39.near), channel_id=1, source_target_pairs={{0,16},{16,0},{32,48},{48,32},{64,80},{80,64},{96,112},{112,96},{1... | collective-permute-start | bytes 786440 | tf_op jit(solution)/shard_map/ppermute | solution.py:443
  50.5 10.7 %collective-permute-start.3 = (f32[128,512]{1,0:T(8,128)S(1)}, f32[128,512]{1,0:T(8,128)S(1)}, u32[]{:S(2)}, u32[]{:S(2)}) collective-permute-start(f32[128,512]{1,0:T(8,128)S(1)} %get-tuple-element.40.far), channel_id=1, source_target_pairs={{16,32},{32,16},{48,64},{64,48},{80,96},{96,80},{112,128},{128,112... | collective-permute-start | bytes 786440 | tf_op jit(solution)/shard_map/ppermute | solution.py:442
  67.2 29.8 %all-to-all-start.2 = ((f32[16,40,512]{2,1,0:T(8,128)}), f32[16,40,512]{2,1,0:T(8,128)S(1)}, u32[]{:S(2)}, u32[]{:S(2)}) async-start(f32[16,40,512]{2,1,0:T(8,128)} %get-tuple-element.48), calls=%async_computation.2 | async-start | bytes 2621440 | tf_op jit(solution)/shard_map/all_to_all | solution.py:439
  77.3 12.3 %collective-permute-start.4 = (f32[128,512]{1,0:T(8,128)S(1)}, f32[128,512]{1,0:T(8,128)S(1)}, u32[]{:S(2)}, u32[]{:S(2)}) collective-permute-start(f32[128,512]{1,0:T(8,128)S(1)} %get-tuple-element.44.near), channel_id=1, source_target_pairs={{0,16},{16,0},{32,48},{48,32},{64,80},{80,64},{96,112},{112,96},{1... | collective-permute-start | bytes 786440 | tf_op jit(solution)/shard_map/ppermute | solution.py:443
  78.2 11.3 %collective-permute-start.5 = (f32[128,512]{1,0:T(8,128)S(1)}, f32[128,512]{1,0:T(8,128)S(1)}, u32[]{:S(2)}, u32[]{:S(2)}) collective-permute-start(f32[128,512]{1,0:T(8,128)S(1)} %get-tuple-element.45.far), channel_id=1, source_target_pairs={{16,32},{32,16},{48,64},{64,48},{80,96},{96,80},{112,128},{128,112... | collective-permute-start | bytes 786440 | tf_op jit(solution)/shard_map/ppermute | solution.py:442

commit v2 on v1

--- a/solution.py
+++ b/solution.py
@@ -147,14 +147,14 @@
     for p in range(SUBS):
         rows = slice(p * CAP, (p + 1) * CAP)
         mhi_v[rows], mlo_v[rows] = split(take_rows(held, starts[p]))
+    for source, near_face, others in ((mhi_v, mhe, mhr), (mlo_v, mle, mlr)):
+        flow.put(source.at[:, pl.ds(0, BORDER)], near_face)
+        flow.put(source.at[:, pl.ds(BORDER, LOC - BORDER)], others)
     for cols, ready in zip(blocks, rhs_in):
         ready.wait()
         dhi, dlo = split(rhs_v[:, cols] * (1.0 / center_value))
         fill(out_v, cols, mm3(mhi_v[...], mlo_v[...], dhi, dlo))
         flow.put(out_v.at[:, :, cols], out.at[:, :, cols])
-    for source, near_face, others in ((mhi_v, mhe, mhr), (mlo_v, mle, mlr)):
-        flow.put(source.at[:, pl.ds(0, BORDER)], near_face)
-        flow.put(source.at[:, pl.ds(BORDER, LOC - BORDER)], others)
     flow.finish()
 
 
@@ -363,37 +363,39 @@
         ahead_in = flow.get(ahead.at[AHEAD], ahead_v)
         starts, total = face_starts(counts)
         blocks = columns(edge.shape[1])
+        for cols in blocks:
+            small_v[:, cols] = arrived_back(cols, arrived, table)
+            part_v[FACE:, cols] = arrived_faces(cols, arrived, starts, total, inner)
+        flow.put(small_v, small)
+        edge_in.wait()
+        flow.put(part_v, part)
         for at, cols in enumerate(blocks):
-            back = arrived_back(cols, arrived, table)
-            small_v[:, cols] = back
-            part_v[FACE:, cols] = arrived_faces(cols, arrived, starts, total, inner)
-            if at == 0:
-                edge_in.wait()
-            product = mm3(mhe[...], mle[...], *split(part_v[:, cols])) - mm(crossed[...], back)
+            product = mm3(mhe[...], mle[...], *split(part_v[:, cols])) - mm(crossed[...], small_v[:, cols])
             if at == 0:
                 ahead_in.wait()
             fill(out_v, cols, ahead_v[:, cols] + scale_r * product)
             flow.put(out_v.at[:, :, cols], out.at[:, :, cols])
-            flow.put(part_v.at[:, cols], part.at[:, cols])
-        flow.put(small_v, small)
         flow.finish()
 
     return body
 
 
-def last_body(arrived, left, edge, table, turned, counts, res, left_v, edge_v, table_v, turned_v, res_v, inner, sems):
+def last_body(arrived, left, edge, table, turned, counts, res, arrived_v, left_v, edge_v, turned_v, res_v, inner, sems):
     flow = Copies(sems)
     starts, total = face_starts(counts)
     blocks = columns(left.shape[1])
-    table_in = [flow.get(table, table_v), flow.get(turned, turned_v)]
+    arrived_in = [flow.get(arrived.at[:, :, cols], arrived_v.at[:, :, cols]) for cols in blocks]
+    turned_in = flow.get(turned, turned_v)
     edge_in = flow.get(edge, edge_v)
     left_in = [flow.get(left.at[:, cols], left_v.at[:, cols]) for cols in blocks]
+    got = []
+    for cols, ready in zip(blocks, arrived_in):
+        ready.wait()
+        got.append((arrived_faces(cols, arrived_v, starts, total, inner), arrived_back(cols, arrived_v, table)))
+    turned_in.wait()
     for at, cols in enumerate(blocks):
-        faces = arrived_faces(cols, arrived, starts, total, inner)
-        if at == 0:
-            for copy in table_in:
-                copy.wait()
-        fix = mm(turned_v[...], arrived_back(cols, arrived, table_v))
+        faces, back = got[at]
+        fix = mm(turned_v[...], back)
         if at == 0:
             edge_in.wait()
         left_in[at].wait()
@@ -536,8 +538,8 @@
         last_body,
         (sds(state),),
         (arrived, made[0], landing, table, turned, counts),
-        (VM,) + (ANY,) * 4 + (SM,),
-        ((state, F32), ((FACE, width), F32), (tables, BF), (turns, BF), (state, F32), (held, F32)),
+        (ANY, ANY, ANY, VM, ANY, SM),
+        ((sent, F32), (state, F32), ((FACE, width), F32), (turns, BF), (state, F32), (held, F32)),
         8,
         100_000_000,
         CRITICAL_GRANT,

time: 103 us -> 103 us (level)
  no operation moved by 1% of the time
where the time goes in v2:
time: 103 us; the launch traced here: 101 us
  Pallas kernels  59.4 us (58%)
  starting transfers between devices  28.7 us (28%)
  waiting for transfers between devices  11.7 us (11%)
  between operations  1.12 us (1%)
    pallas_call x14, Pallas kernels, call(): pl.pallas_call(body, out_shape=outs, in_specs=specs, out_specs=tuple((ANY...  59.4 us
    all_to_all x3, starting transfers between devices, exchange(): return lax.all_to_all(out, 'sub', split_axis=0, concat_axis=0, tiled=True)  17.1 us
    all_to_all x3, waiting for transfers between devices, exchange(): return lax.all_to_all(out, 'sub', split_axis=0, concat_axis=0, tiled=True)  11.7 us
    ppermute x3, starting transfers between devices, swap(): far = lax.ppermute(far, 'clus', pairs(1, clusters))  7.66 us
    ppermute x3, starting transfers between devices, swap(): return (lax.ppermute(near, 'clus', pairs(0, clusters)), far)  3.96 us
  transfers between devices with their start and end apart: 9, of which 3 were waited for; matrix products, arithmetic and copies ran while one was open for 0% of the time, Pallas kernels for 41%

profile of v2, /device:TPU:96, one launch (start us, length us, event | category | flops | bytes accessed | tf_op | source)
XLA Modules:
  0.0 101.0 jit_solution(1843926127718564645)
XLA Ops:
  0.6 5.3 %shard_map.77 = (f32[16,40,512]{2,1,0:T(8,128)}, bf16[288,512]{1,0:T(8,128)(2,1)}, bf16[288,512]{1,0:T(8,128)(2,1)}, bf16[288,384]{1,0:T(8,128)(2,1)}, bf16[288,384]{1,0:T(8,128)(2,1)}) custom-call(f32[896,512]{1,0:T(8,128)} %bitcast.20, f32[896,896]{1,0:T(8,128)} %bitcast.13, f32[24,896]{1,0:T(8,128)} %bitcast.7, s32[1,16]{1,0:T(1,128)} %bitcast.9), custom_call_target="tpu_custom_call" | custom-call | flops 800000000 | bytes 6000000 | tf_op jit(solution)/shard_map/pallas_call | solution.py:55
  5.9 7.1 %all-to-all-start = ((f32[16,40,512]{2,1,0:T(8,128)}), f32[16,40,512]{2,1,0:T(8,128)}, u32[]{:S(2)}, u32[]{:S(2)}) async-start(f32[16,40,512]{2,1,0:T(8,128)} %get-tuple-element.26), calls=%async_computation | async-start | bytes 2621440 | tf_op jit(solution)/shard_map/all_to_all | solution.py:441
  13.0 0.0 copy-start
  13.0 0.0 copy-start.1
  13.0 0.0 copy-start.2
  13.0 0.0 copy-start.3
  13.0 0.0 copy-start.4
  13.1 0.0 copy-start.6
  13.1 3.8 %shard_map.79 = (f32[128,512]{1,0:T(8,128)S(1)}, f32[128,512]{1,0:T(8,128)S(1)}) custom-call(f32[896,512]{1,0:T(8,128)} %bitcast.21, f32[896,896]{1,0:T(8,128)} %bitcast.14), custom_call_target="tpu_custom_call" | custom-call | flops 700000000 | bytes 6000000 | tf_op jit(solution)/shard_map/pallas_call | solution.py:55
  16.8 0.1 collective-permute-start
  16.9 2.1 %collective-permute-start.1 = (f32[128,512]{1,0:T(8,128)S(1)}, f32[128,512]{1,0:T(8,128)S(1)}, u32[]{:S(2)}, u32[]{:S(2)}) collective-permute-start(f32[128,512]{1,0:T(8,128)S(1)} %get-tuple-element.34.far), channel_id=1, source_target_pairs={{16,32},{32,16},{48,64},{64,48},{80,96},{96,80},{112,128},{128,112... | collective-permute-start | bytes 786440 | tf_op jit(solution)/shard_map/ppermute | solution.py:444
  19.1 0.0 copy-done
  19.1 0.0 copy-done.1
  19.1 0.0 copy-done.2
  19.1 0.0 copy-done.3
  19.1 0.0 copy-done.4
  19.1 0.0 copy-done.6
  19.1 3.5 %shard_map.78 = (bf16[64,384]{1,0:T(8,128)(2,1)S(1)}, bf16[896,96]{1,0:T(8,128)(2,1)S(1)}, bf16[288,96]{1,0:T(8,128)(2,1)S(1)}) custom-call(f32[384,384]{1,0:T(8,128)} %bitcast.26, s32[1,384]{1,0:T(1,128)S(1)} %copy-done.6, s32[1,384]{1,0:T(1,128)S(1)} %copy-done.6, f32[24,896]{1,0:T(8,128)S(1)} %bitcast.8, bf16[288,512]{1,0:T(8,128)(2,1)S(1)} %copy-done, ...), custom_call_target="tpu_custom_call" | custom-call | flops 200000000 | bytes 6000000 | tf_op jit(solution)/shard_map/pallas_call | solution.py:55
  22.6 0.0 copy-start.5
  22.6 8.2 %shard_map.80.ahead.base = f32[1184,512]{1,0:T(8,128)} custom-call(f32[896,896]{1,0:T(8,128)} %bitcast.15, f32[128,512]{1,0:T(8,128)S(1)} %get-tuple-element.33.near, f32[128,512]{1,0:T(8,128)S(1)} %get-tuple-element.34.far, f32[896,512]{1,0:T(8,128)} %bitcast.22, bf16[288,512]{1,0:T(8,128)(2,1)S(1)} %copy-done, bf16[288,512]{1,0:T(8,128)(2,1)S(1)} %copy-done.1, ...), custom_call_target="tpu_custom_call" | custom-call | flops 2000000000 | bytes 6000000 | tf_op jit(solution)/shard_map/pallas_call | solution.py:55
  30.8 0.0 collective-permute-done.near_in
  30.8 0.0 collective-permute-done.1.far_in
  30.8 0.1 shard_map.81.edge
  30.9 2.9 %all-to-all-done.arrived = f32[16,40,512]{2,1,0:T(8,128)} async-done(((f32[16,40,512]{2,1,0:T(8,128)}), f32[16,40,512]{2,1,0:T(8,128)}, u32[]{:S(2)}, u32[]{:S(2)}) %all-to-all-start) | async-done | bytes 1310752 | tf_op jit(solution)/shard_map/all_to_all | solution.py:441
  33.9 0.0 copy-done.5
  33.9 4.4 %shard_map.82 = (f32[16,40,512]{2,1,0:T(8,128)}, f32[512,512]{1,0:T(8,128)S(1)}, bf16[96,512]{1,0:T(8,128)(2,1)S(1)}) custom-call(f32[16,40,512]{2,1,0:T(8,128)} %all-to-all-done.arrived, bf16[288,512]{1,0:T(8,128)(2,1)S(1)} %copy-done, bf16[288,512]{1,0:T(8,128)(2,1)S(1)} %copy-done.1, bf16[64,384]{1,0:T(8,128)(2,1)S(1)} %get-tuple-element.31.table, ...), custom_call_target="tpu_custom_call" | custom-call | flops 1000000000 | bytes 6000000 | tf_op jit(solution)/shard_map/pallas_call | solution.py:55
  38.3 4.4 %all-to-all-start.1 = ((f32[16,40,512]{2,1,0:T(8,128)}), f32[16,40,512]{2,1,0:T(8,128)}, u32[]{:S(2)}, u32[]{:S(2)}) async-start(f32[16,40,512]{2,1,0:T(8,128)} %get-tuple-element.35), calls=%async_computation.1 | async-start | bytes 2621440 | tf_op jit(solution)/shard_map/all_to_all | solution.py:441
  42.7 4.6 %shard_map.83 = (f32[896,512]{1,0:T(8,128)}, f32[128,512]{1,0:T(8,128)S(1)}, f32[128,512]{1,0:T(8,128)S(1)}) custom-call(f32[512,512]{1,0:T(8,128)S(1)} %get-tuple-element.36.part, bf16[96,512]{1,0:T(8,128)(2,1)S(1)} %get-tuple-element.37.small, f32[1184,512]{1,0:T(8,128)} %shard_map.80.ahead.base, bf16[896,96]{1,0:T(8,128)(2,1)S(1)} %get-tuple-element.38.turned, ...), custom_call_target="tpu_custom_call" | custom-call | flops 700000000 | bytes 6000000 | tf_op jit(solution)/shard_map/pallas_call | solution.py:55
  47.4 2.9 %collective-permute-start.2 = (f32[128,512]{1,0:T(8,128)S(1)}, f32[128,512]{1,0:T(8,128)S(1)}, u32[]{:S(2)}, u32[]{:S(2)}) collective-permute-start(f32[128,512]{1,0:T(8,128)S(1)} %get-tuple-element.39.near), channel_id=1, source_target_pairs={{0,16},{16,0},{32,48},{48,32},{64,80},{80,64},{96,112},{112,96},{1... | collective-permute-start | bytes 786440 | tf_op jit(solution)/shard_map/ppermute | solution.py:445
  50.3 1.9 %collective-permute-start.3 = (f32[128,512]{1,0:T(8,128)S(1)}, f32[128,512]{1,0:T(8,128)S(1)}, u32[]{:S(2)}, u32[]{:S(2)}) collective-permute-start(f32[128,512]{1,0:T(8,128)S(1)} %get-tuple-element.40.far), channel_id=1, source_target_pairs={{16,32},{32,16},{48,64},{64,48},{80,96},{96,80},{112,128},{128,112... | collective-permute-start | bytes 786440 | tf_op jit(solution)/shard_map/ppermute | solution.py:444
  52.2 8.7 %shard_map.84.ahead.base = f32[1184,512]{1,0:T(8,128)} custom-call(f32[896,896]{1,0:T(8,128)} %bitcast.17, f32[128,512]{1,0:T(8,128)S(1)} %get-tuple-element.39.near, f32[128,512]{1,0:T(8,128)S(1)} %get-tuple-element.40.far, f32[896,512]{1,0:T(8,128)} %get-tuple-element.41.dirn.refs_0_, f32[896,512]{1,0:T(8,128)} %bitcast.23, bf16[288,512]{1,0:T(8,128)(2,1)S(1)} %copy-done, ...), custom_call_target="tpu_custom_call" | custom-call | flops 2000000000 | bytes 6000000 | tf_op jit(solution)/shard_map/pallas_call | solution.py:55
  61.0 0.0 collective-permute-done.2.near_in
  61.0 0.0 collective-permute-done.3.far_in
  61.0 0.1 shard_map.85.edge
  61.1 1.3 %all-to-all-done.1.arrived = f32[16,40,512]{2,1,0:T(8,128)} async-done(((f32[16,40,512]{2,1,0:T(8,128)}), f32[16,40,512]{2,1,0:T(8,128)}, u32[]{:S(2)}, u32[]{:S(2)}) %all-to-all-start.1) | async-done | bytes 1310752 | tf_op jit(solution)/shard_map/all_to_all | solution.py:441
  62.4 4.5 %shard_map.86 = (f32[16,40,512]{2,1,0:T(8,128)}, f32[512,512]{1,0:T(8,128)S(1)}, bf16[96,512]{1,0:T(8,128)(2,1)S(1)}) custom-call(f32[16,40,512]{2,1,0:T(8,128)} %all-to-all-done.1.arrived, bf16[288,512]{1,0:T(8,128)(2,1)S(1)} %copy-done, bf16[288,512]{1,0:T(8,128)(2,1)S(1)} %copy-done.1, bf16[64,384]{1,0:T(8,128)(2,1)S(1)} %get-tuple-element.31.table, ...), custom_call_target="tpu_custom_call" | custom-call | flops 1000000000 | bytes 6000000 | tf_op jit(solution)/shard_map/pallas_call | solution.py:55
  66.9 5.6 %all-to-all-start.2 = ((f32[16,40,512]{2,1,0:T(8,128)}), f32[16,40,512]{2,1,0:T(8,128)S(1)}, u32[]{:S(2)}, u32[]{:S(2)}) async-start(f32[16,40,512]{2,1,0:T(8,128)} %get-tuple-element.48), calls=%async_computation.2 | async-start | bytes 2621440 | tf_op jit(solution)/shard_map/all_to_all | solution.py:441
  72.5 4.7 %shard_map.87 = (f32[896,512]{1,0:T(8,128)}, f32[128,512]{1,0:T(8,128)S(1)}, f32[128,512]{1,0:T(8,128)S(1)}) custom-call(f32[512,512]{1,0:T(8,128)S(1)} %get-tuple-element.42.part, bf16[96,512]{1,0:T(8,128)(2,1)S(1)} %get-tuple-element.43.small, f32[1184,512]{1,0:T(8,128)} %shard_map.84.ahead.base, bf16[896,96]{1,0:T(8,128)(2,1)S(1)} %get-tuple-element.38.turned, ...), custom_call_target="tpu_custom_call" | custom-call | flops 700000000 | bytes 6000000 | tf_op jit(solution)/shard_map/pallas_call | solution.py:55
  77.2 0.9 collective-permute-start.4
  78.1 3.6 %collective-permute-start.5 = (f32[128,512]{1,0:T(8,128)S(1)}, f32[128,512]{1,0:T(8,128)S(1)}, u32[]{:S(2)}, u32[]{:S(2)}) collective-permute-start(f32[128,512]{1,0:T(8,128)S(1)} %get-tuple-element.45.far), channel_id=1, source_target_pairs={{16,32},{32,16},{48,64},{64,48},{80,96},{96,80},{112,128},{128,112... | collective-permute-start | bytes 786440 | tf_op jit(solution)/shard_map/ppermute | solution.py:444
  81.8 7.5 %shard_map.88 = (f32[896,512]{1,0:T(8,128)}, f32[896,512]{1,0:T(8,128)}) custom-call(f32[896,896]{1,0:T(8,128)} %bitcast.19, f32[128,512]{1,0:T(8,128)S(1)} %get-tuple-element.44.near, f32[128,512]{1,0:T(8,128)S(1)} %get-tuple-element.45.far, f32[896,512]{1,0:T(8,128)} %get-tuple-element.46.dirn, f32[896,512]{1,0:T(8,128)} %get-tuple-element.41.dirn.refs_0_, ...), custom_call_target="tpu_custom_call" | custom-call | flops 2000000000 | bytes 6000000 | tf_op jit(solution)/shard_map/pallas_call | solution.py:55
  89.3 0.0 collective-permute-done.4.near_in
  89.3 0.0 collective-permute-done.5.far_in
  89.3 0.1 shard_map.89.edge
  89.4 7.5 %all-to-all-done.2.arrived = f32[16,40,512]{2,1,0:T(8,128)S(1)} async-done(((f32[16,40,512]{2,1,0:T(8,128)}), f32[16,40,512]{2,1,0:T(8,128)S(1)}, u32[]{:S(2)}, u32[]{:S(2)}) %all-to-all-start.2) | async-done | bytes 1310752 | tf_op jit(solution)/shard_map/all_to_all | solution.py:441
  96.9 3.9 %shard_map.90 = f32[896,512]{1,0:T(8,128)} custom-call(f32[16,40,512]{2,1,0:T(8,128)S(1)} %all-to-all-done.2.arrived, f32[896,512]{1,0:T(8,128)} %get-tuple-element.49.left, f32[256,512]{1,0:T(8,128)S(1)} %shard_map.89.edge, bf16[64,384]{1,0:T(8,128)(2,1)S(1)} %get-tuple-element.31.table, bf16[896,96]{1,0:T(8,128)(2,1)S(1)} %get-tuple-element.38.turned, ...), custom_call_target="tpu_custom_call" | custom-call | flops 100000000 | bytes 6000000 | tf_op jit(solution)/shard_map/pallas_call | solution.py:55
Async XLA Ops:
  5.9 28.0 %all-to-all-start = ((f32[16,40,512]{2,1,0:T(8,128)}), f32[16,40,512]{2,1,0:T(8,128)}, u32[]{:S(2)}, u32[]{:S(2)}) async-start(f32[16,40,512]{2,1,0:T(8,128)} %get-tuple-element.26), calls=%async_computation | async-start | bytes 2621440 | tf_op jit(solution)/shard_map/all_to_all | solution.py:441
  13.0 6.1 %copy-start = (bf16[288,512]{1,0:T(8,128)(2,1)S(1)}, bf16[288,512]{1,0:T(8,128)(2,1)}, u32[]{:S(2)}) copy-start(bf16[288,512]{1,0:T(8,128)(2,1)} %get-tuple-element.27.mhe.refs_0_.refs_1_) | copy-start | bytes 884740
  13.0 6.1 %copy-start.1 = (bf16[288,512]{1,0:T(8,128)(2,1)S(1)}, bf16[288,512]{1,0:T(8,128)(2,1)}, u32[]{:S(2)}) copy-start(bf16[288,512]{1,0:T(8,128)(2,1)} %get-tuple-element.28.mle.refs_1_.refs_2_) | copy-start | bytes 884740
  13.0 6.1 %copy-start.2 = (bf16[288,384]{1,0:T(8,128)(2,1)S(1)}, bf16[288,384]{1,0:T(8,128)(2,1)}, u32[]{:S(2)}) copy-start(bf16[288,384]{1,0:T(8,128)(2,1)} %get-tuple-element.29.mhr.refs_2_.refs_3_) | copy-start | bytes 663556
  13.0 6.1 %copy-start.3 = (bf16[288,384]{1,0:T(8,128)(2,1)S(1)}, bf16[288,384]{1,0:T(8,128)(2,1)}, u32[]{:S(2)}) copy-start(bf16[288,384]{1,0:T(8,128)(2,1)} %get-tuple-element.30.mlr.refs_3_.refs_4_) | copy-start | bytes 663556
  13.0 6.1 %copy-start.4 = (f32[1,1,24,896]{3,2,1,0:T(8,128)S(1)}, f32[1,1,24,896]{3,2,1,0:T(8,128)}, u32[]{:S(2)}) copy-start(f32[1,1,24,896]{3,2,1,0:T(8,128)} %param.8) | copy-start | bytes 258052
  13.1 6.1 %copy-start.6 = (s32[1,384]{1,0:T(1,128)S(1)}, s32[1,384]{1,0:T(1,128)}, u32[]{:S(2)}) copy-start(s32[1,384]{1,0:T(1,128)} %place_row.1) | copy-start | bytes 4612
  16.8 14.0 %collective-permute-start = (f32[128,512]{1,0:T(8,128)S(1)}, f32[128,512]{1,0:T(8,128)S(1)}, u32[]{:S(2)}, u32[]{:S(2)}) collective-permute-start(f32[128,512]{1,0:T(8,128)S(1)} %get-tuple-element.33.near), channel_id=1, source_target_pairs={{0,16},{16,0},{32,48},{48,32},{64,80},{80,64},{96,112},{112,96},{1... | collective-permute-start | bytes 786440 | tf_op jit(solution)/shard_map/ppermute | solution.py:445
  16.9 13.9 %collective-permute-start.1 = (f32[128,512]{1,0:T(8,128)S(1)}, f32[128,512]{1,0:T(8,128)S(1)}, u32[]{:S(2)}, u32[]{:S(2)}) collective-permute-start(f32[128,512]{1,0:T(8,128)S(1)} %get-tuple-element.34.far), channel_id=1, source_target_pairs={{16,32},{32,16},{48,64},{64,48},{80,96},{96,80},{112,128},{128,112... | collective-permute-start | bytes 786440 | tf_op jit(solution)/shard_map/ppermute | solution.py:444
  22.6 11.3 %copy-start.5 = (s32[1,1,16]{2,1,0:T(1,128)S(1)}, s32[1,1,16]{2,1,0:T(1,128)}, u32[]{:S(2)}) copy-start(s32[1,1,16]{2,1,0:T(1,128)} %param.11) | copy-start | bytes 196
  38.3 24.0 %all-to-all-start.1 = ((f32[16,40,512]{2,1,0:T(8,128)}), f32[16,40,512]{2,1,0:T(8,128)}, u32[]{:S(2)}, u32[]{:S(2)}) async-start(f32[16,40,512]{2,1,0:T(8,128)} %get-tuple-element.35), calls=%async_computation.1 | async-start | bytes 2621440 | tf_op jit(solution)/shard_map/all_to_all | solution.py:441
  47.4 13.6 %collective-permute-start.2 = (f32[128,512]{1,0:T(8,128)S(1)}, f32[128,512]{1,0:T(8,128)S(1)}, u32[]{:S(2)}, u32[]{:S(2)}) collective-permute-start(f32[128,512]{1,0:T(8,128)S(1)} %get-tuple-element.39.near), channel_id=1, source_target_pairs={{0,16},{16,0},{32,48},{48,32},{64,80},{80,64},{96,112},{112,96},{1... | collective-permute-start | bytes 786440 | tf_op jit(solution)/shard_map/ppermute | solution.py:445
  50.3 10.7 %collective-permute-start.3 = (f32[128,512]{1,0:T(8,128)S(1)}, f32[128,512]{1,0:T(8,128)S(1)}, u32[]{:S(2)}, u32[]{:S(2)}) collective-permute-start(f32[128,512]{1,0:T(8,128)S(1)} %get-tuple-element.40.far), channel_id=1, source_target_pairs={{16,32},{32,16},{48,64},{64,48},{80,96},{96,80},{112,128},{128,112... | collective-permute-start | bytes 786440 | tf_op jit(solution)/shard_map/ppermute | solution.py:444
  66.9 30.0 %all-to-all-start.2 = ((f32[16,40,512]{2,1,0:T(8,128)}), f32[16,40,512]{2,1,0:T(8,128)S(1)}, u32[]{:S(2)}, u32[]{:S(2)}) async-start(f32[16,40,512]{2,1,0:T(8,128)} %get-tuple-element.48), calls=%async_computation.2 | async-start | bytes 2621440 | tf_op jit(solution)/shard_map/all_to_all | solution.py:441
  77.2 12.1 %collective-permute-start.4 = (f32[128,512]{1,0:T(8,128)S(1)}, f32[128,512]{1,0:T(8,128)S(1)}, u32[]{:S(2)}, u32[]{:S(2)}) collective-permute-start(f32[128,512]{1,0:T(8,128)S(1)} %get-tuple-element.44.near), channel_id=1, source_target_pairs={{0,16},{16,0},{32,48},{48,32},{64,80},{80,64},{96,112},{112,96},{1... | collective-permute-start | bytes 786440 | tf_op jit(solution)/shard_map/ppermute | solution.py:445
  78.1 11.2 %collective-permute-start.5 = (f32[128,512]{1,0:T(8,128)S(1)}, f32[128,512]{1,0:T(8,128)S(1)}, u32[]{:S(2)}, u32[]{:S(2)}) collective-permute-start(f32[128,512]{1,0:T(8,128)S(1)} %get-tuple-element.45.far), channel_id=1, source_target_pairs={{16,32},{32,16},{48,64},{64,48},{80,96},{96,80},{112,128},{128,112... | collective-permute-start | bytes 786440 | tf_op jit(solution)/shard_map/ppermute | solution.py:444

commit v3 on v2

--- a/solution.py
+++ b/solution.py
@@ -276,13 +276,12 @@
         before, refs = refs[:olds], refs[olds:]
         parts, refs = (refs[:4], refs[4:]) if not last else ((), refs)
         outs, refs = refs[: 1 + last], refs[1 + last :]
-        (op_v, near_v, far_v, dirn_v), refs = refs[:4], refs[4:]
+        (op_v, dirn_v), refs = refs[:2], refs[2:]
         before_v, refs = refs[:olds], refs[olds:]
-        m_v, refs = (refs[:2], refs[2:]) if not last else ((), refs)
         made, sems = refs[:-1], refs[-1]
         flow = Copies(sems)
         blocks = columns(dirn.shape[1])
-        op_in, dirn_in, before_in, m_in = [], [], [], []
+        op_in, dirn_in, before_in = [], [], []
         for at, cols in enumerate(blocks):
             dirn_in.append(flow.get(dirn.at[:, cols], dirn_v.at[:, cols]))
             if at == 0:
@@ -290,8 +289,6 @@
             before_in.append([flow.get(x.at[:, cols], y.at[:, cols]) for x, y in zip(before, before_v)])
             if at == 0:
                 op_in.append(flow.get(op.at[CHUNKS[1]], op_v.at[CHUNKS[1]]))
-                edges_in = [flow.get(near, near_v), flow.get(far, far_v)]
-                m_in = [] if last else m_copies(flow, parts, *m_v)
         factors = []
         for at, cols in enumerate(blocks):
             dirn_in[at].wait()
@@ -312,19 +309,16 @@
                     for copy in before_in[at]:
                         copy.wait()
                 store(rows, mm3(*factors[part], dhi, dlo))
-            if at == 0:
-                for copy in edges_in:
-                    copy.wait()
-            low, high = pick(near_v[:, cols], far_v[:, cols])
+            low, high = pick(near[:, cols], far[:, cols])
             store(pl.ds(0, FACE), jnp.concatenate([low, high], axis=0))
             if last:
                 made[1][:, cols] = before_v[1][:, cols] * (1.0 / center_value) + before_v[0][:, cols] + dirn_v[:, cols]
                 flow.put(made[1].at[:, cols], outs[1].at[:, cols])
             else:
-                if at == 0:
-                    for copy in m_in:
-                        copy.wait()
-                made[1][:, cols] = mm3(m_v[0][...], m_v[1][...], *split(made[0][:, cols]))
+                mhe, mle, mhr, mlr = parts
+                bhi, blo = split(made[0][:, cols])
+                product = mm3(mhe[...], mle[...], bhi[:BORDER], blo[:BORDER])
+                made[1][:, cols] = product + mm3(mhr[...], mlr[...], bhi[BORDER:], blo[BORDER:])
                 flow.put(made[1].at[:, cols], outs[0].at[AHEAD, cols])
         flow.finish()
 
@@ -468,9 +462,8 @@
             body,
             (sds(state), sds(state)) if last else (sds((LOC + MID + NPAD, width)),),
             (op, near, far, dirn) + before + (() if last else parts),
-            (ANY,) * (4 + len(before) + 4 * (not last)),
-            (((LOC, LOC), F32), (edge, F32), (edge, F32), (state, F32)) + ((state, F32),) * len(before)
-            + (() if last else ((mids, BF), (mids, BF))) + ((state, F32), (state if last else ahead_s, F32)),
+            (ANY, VM, VM, ANY) + (ANY,) * len(before) + (VM,) * (4 * (not last)),
+            (((LOC, LOC), F32), (state, F32)) + ((state, F32),) * len(before) + ((state, F32), (state if last else ahead_s, F32)),
             24,
             2_000_000_000,
             WINDOW_GRANT,

time: 103 us -> 103 us (level)
  waiting for transfers between devices: 11.7 us -> 13 us
    all_to_all x3, waiting for transfers between devices: 11.7 us -> 12.9 us  [exchange(): return lax.all_to_all(out, 'sub', split_axis=0, concat_axis=0, tiled=True)]
  transfers between devices with their start and end apart: 9 -> 9, of which waited for: 3 -> 3; matrix products, arithmetic and copies ran while one was open for 0% -> 0% of each run, Pallas kernels for 41% -> 40%
where the time goes in v3:
time: 103 us; the launch traced here: 101 us
  Pallas kernels  58.5 us (57%)
  starting transfers between devices  28.1 us (27%)
  waiting for transfers between devices  13 us (13%)
  between operations  1.12 us (1%)
    pallas_call x14, Pallas kernels, call(): pl.pallas_call(body, out_shape=outs, in_specs=specs, out_specs=tuple((ANY...  58.5 us
    all_to_all x3, starting transfers between devices, exchange(): return lax.all_to_all(out, 'sub', split_axis=0, concat_axis=0, tiled=True)  16.4 us
    all_to_all x3, waiting for transfers between devices, exchange(): return lax.all_to_all(out, 'sub', split_axis=0, concat_axis=0, tiled=True)  12.9 us
    ppermute x3, starting transfers between devices, swap(): far = lax.ppermute(far, 'clus', pairs(1, clusters))  8.5 us
    ppermute x3, starting transfers between devices, swap(): return (lax.ppermute(near, 'clus', pairs(0, clusters)), far)  3.11 us
  transfers between devices with their start and end apart: 9, of which 3 were waited for; matrix products, arithmetic and copies ran while one was open for 0% of the time, Pallas kernels for 40%

profile of v3, /device:TPU:96, one launch (start us, length us, event | category | flops | bytes accessed | tf_op | source)
XLA Modules:
  0.0 100.6 jit_solution(10812502662197955390)
XLA Ops:
  0.6 5.3 %shard_map.77 = (f32[16,40,512]{2,1,0:T(8,128)}, bf16[288,512]{1,0:T(8,128)(2,1)}, bf16[288,512]{1,0:T(8,128)(2,1)}, bf16[288,384]{1,0:T(8,128)(2,1)}, bf16[288,384]{1,0:T(8,128)(2,1)}) custom-call(f32[896,512]{1,0:T(8,128)} %bitcast.20, f32[896,896]{1,0:T(8,128)} %bitcast.13, f32[24,896]{1,0:T(8,128)} %bitcast.7, s32[1,16]{1,0:T(1,128)} %bitcast.9), custom_call_target="tpu_custom_call" | custom-call | flops 800000000 | bytes 6000000 | tf_op jit(solution)/shard_map/pallas_call | solution.py:55
  5.9 7.1 %all-to-all-start = ((f32[16,40,512]{2,1,0:T(8,128)}), f32[16,40,512]{2,1,0:T(8,128)}, u32[]{:S(2)}, u32[]{:S(2)}) async-start(f32[16,40,512]{2,1,0:T(8,128)} %get-tuple-element.26), calls=%async_computation | async-start | bytes 2621440 | tf_op jit(solution)/shard_map/all_to_all | solution.py:435
  13.0 0.0 copy-start
  13.0 0.0 copy-start.1
  13.0 0.0 copy-start.2
  13.0 0.0 copy-start.3
  13.0 0.0 copy-start.4
  13.1 0.0 copy-start.6
  13.1 3.8 %shard_map.79 = (f32[128,512]{1,0:T(8,128)S(1)}, f32[128,512]{1,0:T(8,128)S(1)}) custom-call(f32[896,512]{1,0:T(8,128)} %bitcast.21, f32[896,896]{1,0:T(8,128)} %bitcast.14), custom_call_target="tpu_custom_call" | custom-call | flops 700000000 | bytes 6000000 | tf_op jit(solution)/shard_map/pallas_call | solution.py:55
  16.8 0.1 collective-permute-start
  16.9 2.1 %collective-permute-start.1 = (f32[128,512]{1,0:T(8,128)S(1)}, f32[128,512]{1,0:T(8,128)S(1)}, u32[]{:S(2)}, u32[]{:S(2)}) collective-permute-start(f32[128,512]{1,0:T(8,128)S(1)} %get-tuple-element.34.far), channel_id=1, source_target_pairs={{16,32},{32,16},{48,64},{64,48},{80,96},{96,80},{112,128},{128,112... | collective-permute-start | bytes 786440 | tf_op jit(solution)/shard_map/ppermute | solution.py:438
  19.1 0.0 copy-done
  19.1 0.0 copy-done.1
  19.1 0.0 copy-done.2
  19.1 0.0 copy-done.3
  19.1 0.0 copy-done.4
  19.1 0.0 copy-done.6
  19.1 3.5 %shard_map.78 = (bf16[64,384]{1,0:T(8,128)(2,1)S(1)}, bf16[896,96]{1,0:T(8,128)(2,1)S(1)}, bf16[288,96]{1,0:T(8,128)(2,1)S(1)}) custom-call(f32[384,384]{1,0:T(8,128)} %bitcast.26, s32[1,384]{1,0:T(1,128)S(1)} %copy-done.6, s32[1,384]{1,0:T(1,128)S(1)} %copy-done.6, f32[24,896]{1,0:T(8,128)S(1)} %bitcast.8, bf16[288,512]{1,0:T(8,128)(2,1)S(1)} %copy-done, ...), custom_call_target="tpu_custom_call" | custom-call | flops 200000000 | bytes 6000000 | tf_op jit(solution)/shard_map/pallas_call | solution.py:55
  22.6 0.0 copy-start.5
  22.6 7.7 %shard_map.80.ahead.base = f32[1184,512]{1,0:T(8,128)} custom-call(f32[896,896]{1,0:T(8,128)} %bitcast.15, f32[128,512]{1,0:T(8,128)S(1)} %get-tuple-element.33.near, f32[128,512]{1,0:T(8,128)S(1)} %get-tuple-element.34.far, f32[896,512]{1,0:T(8,128)} %bitcast.22, bf16[288,512]{1,0:T(8,128)(2,1)S(1)} %copy-done, bf16[288,512]{1,0:T(8,128)(2,1)S(1)} %copy-done.1, ...), custom_call_target="tpu_custom_call" | custom-call | flops 2000000000 | bytes 6000000 | tf_op jit(solution)/shard_map/pallas_call | solution.py:55
  30.3 0.0 collective-permute-done.near_in
  30.4 0.0 collective-permute-done.1.far_in
  30.4 0.1 shard_map.81.edge
  30.4 3.4 %all-to-all-done.arrived = f32[16,40,512]{2,1,0:T(8,128)} async-done(((f32[16,40,512]{2,1,0:T(8,128)}), f32[16,40,512]{2,1,0:T(8,128)}, u32[]{:S(2)}, u32[]{:S(2)}) %all-to-all-start) | async-done | bytes 1310752 | tf_op jit(solution)/shard_map/all_to_all | solution.py:435
  33.9 0.0 copy-done.5
  33.9 4.4 %shard_map.82 = (f32[16,40,512]{2,1,0:T(8,128)}, f32[512,512]{1,0:T(8,128)S(1)}, bf16[96,512]{1,0:T(8,128)(2,1)S(1)}) custom-call(f32[16,40,512]{2,1,0:T(8,128)} %all-to-all-done.arrived, bf16[288,512]{1,0:T(8,128)(2,1)S(1)} %copy-done, bf16[288,512]{1,0:T(8,128)(2,1)S(1)} %copy-done.1, bf16[64,384]{1,0:T(8,128)(2,1)S(1)} %get-tuple-element.31.table, ...), custom_call_target="tpu_custom_call" | custom-call | flops 1000000000 | bytes 6000000 | tf_op jit(solution)/shard_map/pallas_call | solution.py:55
  38.3 4.4 %all-to-all-start.1 = ((f32[16,40,512]{2,1,0:T(8,128)}), f32[16,40,512]{2,1,0:T(8,128)}, u32[]{:S(2)}, u32[]{:S(2)}) async-start(f32[16,40,512]{2,1,0:T(8,128)} %get-tuple-element.35), calls=%async_computation.1 | async-start | bytes 2621440 | tf_op jit(solution)/shard_map/all_to_all | solution.py:435
  42.7 4.6 %shard_map.83 = (f32[896,512]{1,0:T(8,128)}, f32[128,512]{1,0:T(8,128)S(1)}, f32[128,512]{1,0:T(8,128)S(1)}) custom-call(f32[512,512]{1,0:T(8,128)S(1)} %get-tuple-element.36.part, bf16[96,512]{1,0:T(8,128)(2,1)S(1)} %get-tuple-element.37.small, f32[1184,512]{1,0:T(8,128)} %shard_map.80.ahead.base, bf16[896,96]{1,0:T(8,128)(2,1)S(1)} %get-tuple-element.38.turned, ...), custom_call_target="tpu_custom_call" | custom-call | flops 700000000 | bytes 6000000 | tf_op jit(solution)/shard_map/pallas_call | solution.py:55
  47.4 2.5 %collective-permute-start.2 = (f32[128,512]{1,0:T(8,128)S(1)}, f32[128,512]{1,0:T(8,128)S(1)}, u32[]{:S(2)}, u32[]{:S(2)}) collective-permute-start(f32[128,512]{1,0:T(8,128)S(1)} %get-tuple-element.39.near), channel_id=1, source_target_pairs={{0,16},{16,0},{32,48},{48,32},{64,80},{80,64},{96,112},{112,96},{1... | collective-permute-start | bytes 786440 | tf_op jit(solution)/shard_map/ppermute | solution.py:439
  49.8 1.9 %collective-permute-start.3 = (f32[128,512]{1,0:T(8,128)S(1)}, f32[128,512]{1,0:T(8,128)S(1)}, u32[]{:S(2)}, u32[]{:S(2)}) collective-permute-start(f32[128,512]{1,0:T(8,128)S(1)} %get-tuple-element.40.far), channel_id=1, source_target_pairs={{16,32},{32,16},{48,64},{64,48},{80,96},{96,80},{112,128},{128,112... | collective-permute-start | bytes 786440 | tf_op jit(solution)/shard_map/ppermute | solution.py:438
  51.8 8.2 %shard_map.84.ahead.base = f32[1184,512]{1,0:T(8,128)} custom-call(f32[896,896]{1,0:T(8,128)} %bitcast.17, f32[128,512]{1,0:T(8,128)S(1)} %get-tuple-element.39.near, f32[128,512]{1,0:T(8,128)S(1)} %get-tuple-element.40.far, f32[896,512]{1,0:T(8,128)} %get-tuple-element.41.dirn.refs_0_, f32[896,512]{1,0:T(8,128)} %bitcast.23, bf16[288,512]{1,0:T(8,128)(2,1)S(1)} %copy-done, ...), custom_call_target="tpu_custom_call" | custom-call | flops 2000000000 | bytes 6000000 | tf_op jit(solution)/shard_map/pallas_call | solution.py:55
  60.0 0.0 collective-permute-done.2.near_in
  60.0 0.0 collective-permute-done.3.far_in
  60.0 0.1 shard_map.85.edge
  60.1 3.2 %all-to-all-done.1.arrived = f32[16,40,512]{2,1,0:T(8,128)} async-done(((f32[16,40,512]{2,1,0:T(8,128)}), f32[16,40,512]{2,1,0:T(8,128)}, u32[]{:S(2)}, u32[]{:S(2)}) %all-to-all-start.1) | async-done | bytes 1310752 | tf_op jit(solution)/shard_map/all_to_all | solution.py:435
  63.3 4.5 %shard_map.86 = (f32[16,40,512]{2,1,0:T(8,128)}, f32[512,512]{1,0:T(8,128)S(1)}, bf16[96,512]{1,0:T(8,128)(2,1)S(1)}) custom-call(f32[16,40,512]{2,1,0:T(8,128)} %all-to-all-done.1.arrived, bf16[288,512]{1,0:T(8,128)(2,1)S(1)} %copy-done, bf16[288,512]{1,0:T(8,128)(2,1)S(1)} %copy-done.1, bf16[64,384]{1,0:T(8,128)(2,1)S(1)} %get-tuple-element.31.table, ...), custom_call_target="tpu_custom_call" | custom-call | flops 1000000000 | bytes 6000000 | tf_op jit(solution)/shard_map/pallas_call | solution.py:55
  67.8 5.0 %all-to-all-start.2 = ((f32[16,40,512]{2,1,0:T(8,128)}), f32[16,40,512]{2,1,0:T(8,128)S(1)}, u32[]{:S(2)}, u32[]{:S(2)}) async-start(f32[16,40,512]{2,1,0:T(8,128)} %get-tuple-element.48), calls=%async_computation.2 | async-start | bytes 2621440 | tf_op jit(solution)/shard_map/all_to_all | solution.py:435
  72.8 4.7 %shard_map.87 = (f32[896,512]{1,0:T(8,128)}, f32[128,512]{1,0:T(8,128)S(1)}, f32[128,512]{1,0:T(8,128)S(1)}) custom-call(f32[512,512]{1,0:T(8,128)S(1)} %get-tuple-element.42.part, bf16[96,512]{1,0:T(8,128)(2,1)S(1)} %get-tuple-element.43.small, f32[1184,512]{1,0:T(8,128)} %shard_map.84.ahead.base, bf16[896,96]{1,0:T(8,128)(2,1)S(1)} %get-tuple-element.38.turned, ...), custom_call_target="tpu_custom_call" | custom-call | flops 700000000 | bytes 6000000 | tf_op jit(solution)/shard_map/pallas_call | solution.py:55
  77.5 0.6 collective-permute-start.4
  78.0 4.5 %collective-permute-start.5 = (f32[128,512]{1,0:T(8,128)S(1)}, f32[128,512]{1,0:T(8,128)S(1)}, u32[]{:S(2)}, u32[]{:S(2)}) collective-permute-start(f32[128,512]{1,0:T(8,128)S(1)} %get-tuple-element.45.far), channel_id=1, source_target_pairs={{16,32},{32,16},{48,64},{64,48},{80,96},{96,80},{112,128},{128,112... | collective-permute-start | bytes 786440 | tf_op jit(solution)/shard_map/ppermute | solution.py:438
  82.5 7.6 %shard_map.88 = (f32[896,512]{1,0:T(8,128)}, f32[896,512]{1,0:T(8,128)}) custom-call(f32[896,896]{1,0:T(8,128)} %bitcast.19, f32[128,512]{1,0:T(8,128)S(1)} %get-tuple-element.44.near, f32[128,512]{1,0:T(8,128)S(1)} %get-tuple-element.45.far, f32[896,512]{1,0:T(8,128)} %get-tuple-element.46.dirn, f32[896,512]{1,0:T(8,128)} %get-tuple-element.41.dirn.refs_0_, ...), custom_call_target="tpu_custom_call" | custom-call | flops 2000000000 | bytes 6000000 | tf_op jit(solution)/shard_map/pallas_call | solution.py:55
  90.1 0.0 collective-permute-done.4.near_in
  90.1 0.0 collective-permute-done.5.far_in
  90.1 0.1 shard_map.89.edge
  90.2 6.3 %all-to-all-done.2.arrived = f32[16,40,512]{2,1,0:T(8,128)S(1)} async-done(((f32[16,40,512]{2,1,0:T(8,128)}), f32[16,40,512]{2,1,0:T(8,128)S(1)}, u32[]{:S(2)}, u32[]{:S(2)}) %all-to-all-start.2) | async-done | bytes 1310752 | tf_op jit(solution)/shard_map/all_to_all | solution.py:435
  96.5 3.9 %shard_map.90 = f32[896,512]{1,0:T(8,128)} custom-call(f32[16,40,512]{2,1,0:T(8,128)S(1)} %all-to-all-done.2.arrived, f32[896,512]{1,0:T(8,128)} %get-tuple-element.49.left, f32[256,512]{1,0:T(8,128)S(1)} %shard_map.89.edge, bf16[64,384]{1,0:T(8,128)(2,1)S(1)} %get-tuple-element.31.table, bf16[896,96]{1,0:T(8,128)(2,1)S(1)} %get-tuple-element.38.turned, ...), custom_call_target="tpu_custom_call" | custom-call | flops 100000000 | bytes 6000000 | tf_op jit(solution)/shard_map/pallas_call | solution.py:55
Async XLA Ops:
  5.9 28.0 %all-to-all-start = ((f32[16,40,512]{2,1,0:T(8,128)}), f32[16,40,512]{2,1,0:T(8,128)}, u32[]{:S(2)}, u32[]{:S(2)}) async-start(f32[16,40,512]{2,1,0:T(8,128)} %get-tuple-element.26), calls=%async_computation | async-start | bytes 2621440 | tf_op jit(solution)/shard_map/all_to_all | solution.py:435
  13.0 6.1 %copy-start = (bf16[288,512]{1,0:T(8,128)(2,1)S(1)}, bf16[288,512]{1,0:T(8,128)(2,1)}, u32[]{:S(2)}) copy-start(bf16[288,512]{1,0:T(8,128)(2,1)} %get-tuple-element.27.mhe.refs_0_.refs_1_) | copy-start | bytes 884740
  13.0 6.1 %copy-start.1 = (bf16[288,512]{1,0:T(8,128)(2,1)S(1)}, bf16[288,512]{1,0:T(8,128)(2,1)}, u32[]{:S(2)}) copy-start(bf16[288,512]{1,0:T(8,128)(2,1)} %get-tuple-element.28.mle.refs_1_.refs_2_) | copy-start | bytes 884740
  13.0 6.1 %copy-start.2 = (bf16[288,384]{1,0:T(8,128)(2,1)S(1)}, bf16[288,384]{1,0:T(8,128)(2,1)}, u32[]{:S(2)}) copy-start(bf16[288,384]{1,0:T(8,128)(2,1)} %get-tuple-element.29.mhr.refs_2_.refs_3_) | copy-start | bytes 663556
  13.0 6.1 %copy-start.3 = (bf16[288,384]{1,0:T(8,128)(2,1)S(1)}, bf16[288,384]{1,0:T(8,128)(2,1)}, u32[]{:S(2)}) copy-start(bf16[288,384]{1,0:T(8,128)(2,1)} %get-tuple-element.30.mlr.refs_3_.refs_4_) | copy-start | bytes 663556
  13.0 6.1 %copy-start.4 = (f32[1,1,24,896]{3,2,1,0:T(8,128)S(1)}, f32[1,1,24,896]{3,2,1,0:T(8,128)}, u32[]{:S(2)}) copy-start(f32[1,1,24,896]{3,2,1,0:T(8,128)} %param.8) | copy-start | bytes 258052
  13.1 6.1 %copy-start.6 = (s32[1,384]{1,0:T(1,128)S(1)}, s32[1,384]{1,0:T(1,128)}, u32[]{:S(2)}) copy-start(s32[1,384]{1,0:T(1,128)} %place_row.1) | copy-start | bytes 4612
  16.8 13.5 %collective-permute-start = (f32[128,512]{1,0:T(8,128)S(1)}, f32[128,512]{1,0:T(8,128)S(1)}, u32[]{:S(2)}, u32[]{:S(2)}) collective-permute-start(f32[128,512]{1,0:T(8,128)S(1)} %get-tuple-element.33.near), channel_id=1, source_target_pairs={{0,16},{16,0},{32,48},{48,32},{64,80},{80,64},{96,112},{112,96},{1... | collective-permute-start | bytes 786440 | tf_op jit(solution)/shard_map/ppermute | solution.py:439
  16.9 13.4 %collective-permute-start.1 = (f32[128,512]{1,0:T(8,128)S(1)}, f32[128,512]{1,0:T(8,128)S(1)}, u32[]{:S(2)}, u32[]{:S(2)}) collective-permute-start(f32[128,512]{1,0:T(8,128)S(1)} %get-tuple-element.34.far), channel_id=1, source_target_pairs={{16,32},{32,16},{48,64},{64,48},{80,96},{96,80},{112,128},{128,112... | collective-permute-start | bytes 786440 | tf_op jit(solution)/shard_map/ppermute | solution.py:438
  22.6 11.3 %copy-start.5 = (s32[1,1,16]{2,1,0:T(1,128)S(1)}, s32[1,1,16]{2,1,0:T(1,128)}, u32[]{:S(2)}) copy-start(s32[1,1,16]{2,1,0:T(1,128)} %param.11) | copy-start | bytes 196
  38.3 25.0 %all-to-all-start.1 = ((f32[16,40,512]{2,1,0:T(8,128)}), f32[16,40,512]{2,1,0:T(8,128)}, u32[]{:S(2)}, u32[]{:S(2)}) async-start(f32[16,40,512]{2,1,0:T(8,128)} %get-tuple-element.35), calls=%async_computation.1 | async-start | bytes 2621440 | tf_op jit(solution)/shard_map/all_to_all | solution.py:435
  47.4 12.6 %collective-permute-start.2 = (f32[128,512]{1,0:T(8,128)S(1)}, f32[128,512]{1,0:T(8,128)S(1)}, u32[]{:S(2)}, u32[]{:S(2)}) collective-permute-start(f32[128,512]{1,0:T(8,128)S(1)} %get-tuple-element.39.near), channel_id=1, source_target_pairs={{0,16},{16,0},{32,48},{48,32},{64,80},{80,64},{96,112},{112,96},{1... | collective-permute-start | bytes 786440 | tf_op jit(solution)/shard_map/ppermute | solution.py:439
  49.8 10.2 %collective-permute-start.3 = (f32[128,512]{1,0:T(8,128)S(1)}, f32[128,512]{1,0:T(8,128)S(1)}, u32[]{:S(2)}, u32[]{:S(2)}) collective-permute-start(f32[128,512]{1,0:T(8,128)S(1)} %get-tuple-element.40.far), channel_id=1, source_target_pairs={{16,32},{32,16},{48,64},{64,48},{80,96},{96,80},{112,128},{128,112... | collective-permute-start | bytes 786440 | tf_op jit(solution)/shard_map/ppermute | solution.py:438
  67.8 28.7 %all-to-all-start.2 = ((f32[16,40,512]{2,1,0:T(8,128)}), f32[16,40,512]{2,1,0:T(8,128)S(1)}, u32[]{:S(2)}, u32[]{:S(2)}) async-start(f32[16,40,512]{2,1,0:T(8,128)} %get-tuple-element.48), calls=%async_computation.2 | async-start | bytes 2621440 | tf_op jit(solution)/shard_map/all_to_all | solution.py:435
  77.5 12.7 %collective-permute-start.4 = (f32[128,512]{1,0:T(8,128)S(1)}, f32[128,512]{1,0:T(8,128)S(1)}, u32[]{:S(2)}, u32[]{:S(2)}) collective-permute-start(f32[128,512]{1,0:T(8,128)S(1)} %get-tuple-element.44.near), channel_id=1, source_target_pairs={{0,16},{16,0},{32,48},{48,32},{64,80},{80,64},{96,112},{112,96},{1... | collective-permute-start | bytes 786440 | tf_op jit(solution)/shard_map/ppermute | solution.py:439
  78.0 12.1 %collective-permute-start.5 = (f32[128,512]{1,0:T(8,128)S(1)}, f32[128,512]{1,0:T(8,128)S(1)}, u32[]{:S(2)}, u32[]{:S(2)}) collective-permute-start(f32[128,512]{1,0:T(8,128)S(1)} %get-tuple-element.45.far), channel_id=1, source_target_pairs={{16,32},{32,16},{48,64},{64,48},{80,96},{96,80},{112,128},{128,112... | collective-permute-start | bytes 786440 | tf_op jit(solution)/shard_map/ppermute | solution.py:438
